TPU v7x, 256 devices: a whole 4x4x8 slice. The times are simulated.
256 devices in a mesh: seq: 128 (over x, z, y), head: 2 (over core).
Axes of the slice: x: 4, y: 4, z: 8, core: 2. Of those that a mesh axis runs over, the one named last changes fastest.
Arguments:
- q_raster: bfloat16 [65536, 2048], P('seq', 'head'), may hold values from -11 to 11
- k_raster: bfloat16 [65536, 2048], P('seq', 'head'), may hold values from -11 to 11
- v_raster: bfloat16 [65536, 2048], P('seq', 'head'), may hold values from -15 to 15
- hilbert_order: int32 [65536], P('seq'), may hold values from 0 to 65535, as said below
- key_blocks: int32 [128, 8], P('seq'), may hold values from 0 to 127, as said below
- out_weight: bfloat16 [2048, 2048], P('head'), may hold values from -0.125 to 0.125
Outputs:
- projected: bfloat16 [65536, 2048], P(('seq', 'head'))
Inputs may be any that keep to these rules, and one draw needn't show every extreme that they name: `hilbert_order`: the image is 256 patches wide, and raster row r is line r // 256, column r % 256. Aligned range t of 1024 positions holds, in some order, exactly the rows of the square tile of lines (t // 8) * 32 onward and columns (t % 8) * 32 onward, 32 of each. `key_blocks`: row b lists b, b - 1 and b + 1 (modulo 128) in slots 0, 1 and 2, then other blocks; the 8 entries of a row are distinct.
All inputs are finite; a program needn't handle non-finite values.
Results may differ from a plain program's by a relative error of at most 0.0053.
Values may be sent and summed in bfloat16 or wider, within the bound.
No kernel may reach another device: no remote copies, remote signals or barrier semaphores. Data moves between devices by JAX's collectives and lax.ppermute only.
A program may use at most 128 MiB of HBM per device.

v0:
```python
import math

import jax
import jax.numpy as jnp
from jax import lax
from jax.sharding import PartitionSpec as P

TILE = 32
TCOLS = 8
HD = 128


def partner(value, axis, apart):
    return lax.ppermute(value, axis, [(i, i ^ 1 << apart) for i in range(lax.axis_size(axis))])


def body(q_raster, k_raster, v_raster, hilbert_order, key_blocks, out_weight):
    seq_count = lax.axis_size("seq")
    seq_pos = lax.axis_index("seq")
    block_rows, feat_width = q_raster.shape
    image_width = TILE * TCOLS
    line_count = block_rows // image_width
    seg_rows = line_count * TILE
    stacked = jnp.stack([q_raster, k_raster, v_raster], axis=0)
    slots = stacked.reshape(3, line_count, TCOLS, TILE, feat_width)
    slots = jnp.transpose(slots, (2, 0, 1, 3, 4)).reshape(TCOLS, 3, seg_rows, feat_width)
    pair_index = seq_pos // 2 % TCOLS
    for section in range(TCOLS.bit_length() - 1):
        low_span = 1 << section
        shaped = slots.reshape(TCOLS // (2 * low_span), 2, low_span, 3, seg_rows, feat_width)
        my_bit = pair_index // low_span % 2
        outgoing = jnp.where(my_bit == 0, shaped[:, 1], shaped[:, 0])
        incoming = partner(outgoing, "seq", section + 1)
        kept = jnp.where(my_bit == 0, shaped[:, 0], shaped[:, 1])
        first_half = jnp.where(my_bit == 0, kept, incoming)
        second_half = jnp.where(my_bit == 0, incoming, kept)
        slots = jnp.stack([first_half, second_half], axis=1).reshape(TCOLS, 3, seg_rows, feat_width)
    partner_slots = partner(slots, "seq", 0)
    is_even = seq_pos % 2 == 0
    even_slots = jnp.where(is_even, slots, partner_slots)
    odd_slots = jnp.where(is_even, partner_slots, slots)
    tile_rows = jnp.stack([even_slots, odd_slots], axis=1)
    tile_rows = jnp.transpose(tile_rows, (2, 0, 1, 3, 4)).reshape(3, TILE * TILE, feat_width)
    in_tile = hilbert_order // image_width % TILE * TILE + hilbert_order % image_width % TILE
    query = jnp.take(tile_rows[0], in_tile, axis=0)
    keys_here = jnp.take(tile_rows[1], in_tile, axis=0)
    values_here = jnp.take(tile_rows[2], in_tile, axis=0)
    slice_rows = block_rows // seq_count
    spread_k, spread_v = (
        lax.all_to_all(
            keys_here.reshape(1, block_rows, feat_width),
            "seq",
            split_axis=1,
            concat_axis=0,
            tiled=True,
        ),
        lax.all_to_all(
            values_here.reshape(1, block_rows, feat_width),
            "seq",
            split_axis=1,
            concat_axis=0,
            tiled=True,
        ),
    )
    lists = lax.all_gather(key_blocks, "seq", axis=0, tiled=True)
    chosen = jnp.transpose(lists)
    slot_count = chosen.shape[0]
    send_k = spread_k[chosen].reshape(slot_count, seq_count * slice_rows, feat_width)
    send_v = spread_v[chosen].reshape(slot_count, seq_count * slice_rows, feat_width)
    key_rows = lax.all_to_all(send_k, "seq", split_axis=1, concat_axis=1, tiled=True).reshape(
        -1, feat_width
    )
    value_rows = lax.all_to_all(send_v, "seq", split_axis=1, concat_axis=1, tiled=True).reshape(
        -1, feat_width
    )
    score_scale = 1.0 / math.sqrt(HD)
    heads_here = feat_width // HD

    def head_stride(head_index, attended_acc):
        column_start = head_index * HD
        query_head = lax.dynamic_slice_in_dim(query, column_start, HD, 1)
        key_head = lax.dynamic_slice_in_dim(key_rows, column_start, HD, 1)
        value_head = lax.dynamic_slice_in_dim(value_rows, column_start, HD, 1)
        scores = (
            lax.dot_general(
                query_head, key_head, (((1,), (1,)), ((), ())), preferred_element_type=jnp.float32
            )
            * score_scale
        )
        row_max = jnp.max(scores, axis=1, keepdims=True)
        weights = jnp.exp(scores - row_max)
        totals = jnp.sum(weights, axis=1, keepdims=True)
        mixed_head = (
            jnp.dot(weights.astype(jnp.bfloat16), value_head, preferred_element_type=jnp.float32)
            / totals
        )
        return lax.dynamic_update_slice_in_dim(
            attended_acc, mixed_head.astype(jnp.bfloat16), column_start, 1
        )

    attended = lax.fori_loop(
        0, heads_here, head_stride, jnp.zeros((block_rows, feat_width), jnp.bfloat16)
    )
    projected = lax.psum_scatter(
        jnp.dot(attended, out_weight, preferred_element_type=jnp.float32),
        "head",
        scatter_dimension=0,
        tiled=True,
    )
    return projected.astype(jnp.bfloat16)


def solution(mesh):
    placed = (
        P("seq", "head"),
        P("seq", "head"),
        P("seq", "head"),
        P("seq"),
        P("seq", None),
        P("head", None),
    )
    return jax.shard_map(
        body, mesh=mesh, in_specs=placed, out_specs=P(("seq", "head"), None), check_vma=False
    )
```

profile of v0, /device:TPU:1, one launch (start us, length us, event | category | flops | bytes accessed | tf_op | source)
XLA Modules:
  0.0 1138.6 jit_solution(4535168232681721219)
XLA Ops:
  14.2 33.4 %collective-permute-done = bf16[4,1,3,64,1024]{4,3,2,0,1:T(8,128)(2,1)} collective-permute-done((bf16[4,1,3,64,1024]{4,3,2,0,1:T(8,128)(2,1)}, bf16[4,1,3,64,1024]{4,3,2,0,1:T(8,128)(2,1)}, u32[]{:S(2)}, u32[]{:S(2)}) %collective-permute-start) | collective-permute-done | bytes 1572896 | tf_op jit(solution)/shard_map/ppermute | solution.py:14
  53.3 33.1 %collective-permute-done.1 = bf16[2,2,3,64,1024]{4,3,2,0,1:T(8,128)(2,1)S(1)} collective-permute-done((bf16[2,2,3,64,1024]{4,3,2,0,1:T(8,128)(2,1)S(1)}, bf16[2,2,3,64,1024]{4,3,2,0,1:T(8,128)(2,1)S(1)}, u32[]{:S(2)}, u32[]{:S(2)}) %collective-permute-start.1) | collective-permute-done | bytes 1572896 | tf_op jit(solution)/shard_map/ppermute | solution.py:14
  92.6 67.5 %collective-permute-done.2 = bf16[1,4,3,64,1024]{4,3,2,1,0:T(8,128)(2,1)S(1)} collective-permute-done((bf16[1,4,3,64,1024]{4,3,2,1,0:T(8,128)(2,1)S(1)}, bf16[1,4,3,64,1024]{4,3,2,1,0:T(8,128)(2,1)S(1)}, u32[]{:S(2)}, u32[]{:S(2)}) %collective-permute-start.2) | collective-permute-done | bytes 1572896 | tf_op jit(solution)/shard_map/ppermute | solution.py:14
  162.6 66.8 %collective-permute-done.3 = bf16[8,3,64,1024]{3,2,0,1:T(8,128)(2,1)} collective-permute-done((bf16[8,3,64,1024]{3,2,0,1:T(8,128)(2,1)S(1)}, bf16[8,3,64,1024]{3,2,0,1:T(8,128)(2,1)}, u32[]{:S(2)}, u32[]{:S(2)}) %collective-permute-start.3) | collective-permute-done | bytes 3145760 | tf_op jit(solution)/shard_map/ppermute | solution.py:14
  254.3 7.8 reduce.4
  264.8 16.2 %all-to-all-start = ((bf16[128,2,2048]{2,1,0:T(2,128)(2,1)}), bf16[128,2,2048]{2,1,0:T(2,128)(2,1)}, u32[]{:S(2)}, u32[]{:S(2)}) async-start(bf16[128,2,2048]{2,1,0:T(2,128)(2,1)} %reshape.210), calls=%async_computation | async-start | bytes 2097152 | tf_op jit(solution)/shard_map/all_to_all | solution.py:50
  290.9 15.5 %all-to-all-done = bf16[128,2,2048]{2,1,0:T(2,128)(2,1)} async-done(((bf16[128,2,2048]{2,1,0:T(2,128)(2,1)}), bf16[128,2,2048]{2,1,0:T(2,128)(2,1)}, u32[]{:S(2)}, u32[]{:S(2)}) %all-to-all-start) | async-done | bytes 1048608 | tf_op jit(solution)/shard_map/all_to_all | solution.py:50
  306.4 9.2 all-to-all-start.2
  315.6 296.9 %all-gather = s32[128,1,8]{2,1,0:T(1,128)S(1)} all-gather(s32[1,1,8]{2,1,0:T(1,128)S(1)} %bitcast.160), channel_id=1, replica_groups=mesh['seq'=128,'head'=2] {'seq'}, dimensions={0}, use_global_device_ids=true | all-gather | bytes 4128 | tf_op jit(solution)/shard_map/all_gather | solution.py:65
  619.2 7.1 bitcast_reduce_fusion.1
  627.7 15.4 %gather_fusion = bf16[1024,4,1024]{2,1,0:T(4,128)(2,1)} fusion(bf16[128,4,1024]{2,1,0:T(4,128)(2,1)S(1)} %all_to_all.25, s32[1024]{0:T(1024)S(1)} %fusion.28), kind=kCustom, calls=%fused_computation.3 | custom fusion | bytes 16781312 | tf_op jit(solution)/shard_map/gather | solution.py:68
  643.1 12.9 %reshape.146 = bf16[8,512,1024]{2,1,0:T(8,128)(2,1)} reshape(bf16[1024,4,1024]{2,1,0:T(4,128)(2,1)} %gather_fusion) | data formatting | bytes 16777216 | tf_op jit(solution)/shard_map/reshape | solution.py:68
  656.0 11.3 copy.76
  667.3 7.7 all-to-all-start.1
  682.7 15.4 %gather_fusion.1 = bf16[1024,4,1024]{2,1,0:T(4,128)(2,1)} fusion(bf16[128,4,1024]{2,1,0:T(4,128)(2,1)S(1)} %all_to_all.28, s32[1024]{0:T(1024)S(1)} %fusion.28), kind=kCustom, calls=%fused_computation.4 | custom fusion | bytes 16781312 | tf_op jit(solution)/shard_map/gather | solution.py:69
  698.1 12.7 %reshape.149 = bf16[8,512,1024]{2,1,0:T(8,128)(2,1)} reshape(bf16[1024,4,1024]{2,1,0:T(4,128)(2,1)} %gather_fusion.1) | data formatting | bytes 16777216 | tf_op jit(solution)/shard_map/reshape | solution.py:69
  710.8 11.3 copy.79
  722.1 79.2 %all-to-all-done.1 = bf16[8,512,1024]{2,0,1:T(8,128)(2,1)} async-done(((bf16[8,512,1024]{2,0,1:T(8,128)(2,1)}), bf16[8,512,1024]{2,0,1:T(8,128)(2,1)}, u32[]{:S(2)}, u32[]{:S(2)}) %all-to-all-start.1) | async-done | bytes 8388640 | tf_op jit(solution)/shard_map/all_to_all | solution.py:70
  801.3 12.4 %all-to-all-start.3 = ((bf16[8,512,1024]{2,0,1:T(8,128)(2,1)}), bf16[8,512,1024]{2,0,1:T(8,128)(2,1)}, u32[]{:S(2)}, u32[]{:S(2)}) async-start(bf16[8,512,1024]{2,0,1:T(8,128)(2,1)} %copy.79), calls=%async_computation.3 | async-start | bytes 16777216 | tf_op jit(solution)/shard_map/all_to_all | solution.py:73
  814.1 11.3 copy.77
  825.4 155.7 %all-to-all-done.3 = bf16[8,512,1024]{2,0,1:T(8,128)(2,1)} async-done(((bf16[8,512,1024]{2,0,1:T(8,128)(2,1)}), bf16[8,512,1024]{2,0,1:T(8,128)(2,1)}, u32[]{:S(2)}, u32[]{:S(2)}) %all-to-all-start.3) | async-done | bytes 8388640 | tf_op jit(solution)/shard_map/all_to_all | solution.py:73
  981.1 11.3 copy.80
  992.5 55.8 %while.13 = (s32[]{:T(128)}, bf16[512,1024]{1,0:T(8,128)(2,1)S(1)}, bf16[512,1024]{1,0:T(8,128)(2,1)}, bf16[4096,1024]{1,0:T(8,128)(2,1)}, bf16[4096,1024]{1,0:T...) while((s32[]{:T(128)}, bf16[512,1024]{1,0:T(8,128)(2,1)S(1)}, bf16[512,1024]{1,0:T(8,128)(2,1)}, ...), condition=%wide.region_3.5_spmd, body=%wide.region_0.4_spmd.sunk | while | flops 1090649088 | bytes 27537548 | solution.py:101
  1054.9 73.7 %reduce-scatter.2.cloned.1.call-done = f32[256,2048]{1,0:T(8,128)} async-done(((f32[512,2048]{1,0:T(8,128)}), f32[256,2048]{1,0:T(8,128)}) %reduce-scatter.2.cloned.1.call-update) | async-done | bytes 2097168 | tf_op jit(solution)/shard_map/reduce_scatter | solution.py:104
  (75 shorter events, 140.1 us)
Async XLA Ops:
  10.4 37.1 %collective-permute-start = (bf16[4,1,3,64,1024]{4,3,2,0,1:T(8,128)(2,1)}, bf16[4,1,3,64,1024]{4,3,2,0,1:T(8,128)(2,1)}, u32[]{:S(2)}, u32[]{:S(2)}) collective-permute-start(bf16[4,1,3,64,1024]{4,3,2,0,1:T(8,128)(2,1)} %fusion.20), channel_id=1, source_target_pairs={{0,4},{2,6},{4,0},{6,2},{8,12},{10,14},{12,8},{14,10},{16,20},{18,... | collective-permute-start | bytes 4718600 | tf_op jit(solution)/shard_map/ppermute | solution.py:14
  49.2 1.2 copy-start
  49.2 1.6 copy-start.1
  50.9 35.5 %collective-permute-start.1 = (bf16[2,2,3,64,1024]{4,3,2,0,1:T(8,128)(2,1)S(1)}, bf16[2,2,3,64,1024]{4,3,2,0,1:T(8,128)(2,1)S(1)}, u32[]{:S(2)}, u32[]{:S(2)}) collective-permute-start(bf16[2,2,3,64,1024]{4,3,2,0,1:T(8,128)(2,1)S(1)} %fusion.21), channel_id=1, source_target_pairs={{0,8},{2,10},{4,12},{6,14},{8,0},{10,2},{12,4},{14,6},{16,24},{18,... | collective-permute-start | bytes 4718600 | tf_op jit(solution)/shard_map/ppermute | solution.py:14
  89.6 70.5 %collective-permute-start.2 = (bf16[1,4,3,64,1024]{4,3,2,1,0:T(8,128)(2,1)S(1)}, bf16[1,4,3,64,1024]{4,3,2,1,0:T(8,128)(2,1)S(1)}, u32[]{:S(2)}, u32[]{:S(2)}) collective-permute-start(bf16[1,4,3,64,1024]{4,3,2,1,0:T(8,128)(2,1)S(1)} %fusion.22), channel_id=1, source_target_pairs={{0,16},{2,18},{4,20},{6,22},{8,24},{10,26},{12,28},{14,30},{16,0},... | collective-permute-start | bytes 4718600 | tf_op jit(solution)/shard_map/ppermute | solution.py:14
  160.7 1.8 copy-start.2
  161.1 68.2 %collective-permute-start.3 = (bf16[8,3,64,1024]{3,2,0,1:T(8,128)(2,1)S(1)}, bf16[8,3,64,1024]{3,2,0,1:T(8,128)(2,1)}, u32[]{:S(2)}, u32[]{:S(2)}) collective-permute-start(bf16[8,3,64,1024]{3,2,0,1:T(8,128)(2,1)S(1)} %bitcast.152), channel_id=1, source_target_pairs={{0,2},{2,0},{4,6},{6,4},{8,10},{10,8},{12,14},{14,12},{16,18},{18,... | collective-permute-start | bytes 9437192 | tf_op jit(solution)/shard_map/ppermute | solution.py:14
  264.8 41.7 %all-to-all-start = ((bf16[128,2,2048]{2,1,0:T(2,128)(2,1)}), bf16[128,2,2048]{2,1,0:T(2,128)(2,1)}, u32[]{:S(2)}, u32[]{:S(2)}) async-start(bf16[128,2,2048]{2,1,0:T(2,128)(2,1)} %reshape.210), calls=%async_computation | async-start | bytes 2097152 | tf_op jit(solution)/shard_map/all_to_all | solution.py:50
  282.6 33.0 %copy-start.3 = (s32[1,8]{1,0:T(1,128)S(1)}, s32[1,8]{1,0:T(1,128)}, u32[]{:S(2)}) copy-start(s32[1,8]{1,0:T(1,128)} %param.14) | copy-start | bytes 100
  306.4 360.9 %all-to-all-start.2 = ((bf16[128,2,2048]{2,1,0:T(2,128)(2,1)}), bf16[128,2,2048]{2,1,0:T(2,128)(2,1)S(1)}, u32[]{:S(2)}, u32[]{:S(2)}) async-start(bf16[128,2,2048]{2,1,0:T(2,128)(2,1)} %reshape.212), calls=%async_computation.2 | async-start | bytes 2097152 | tf_op jit(solution)/shard_map/all_to_all | solution.py:57
  667.3 134.0 %all-to-all-start.1 = ((bf16[8,512,1024]{2,0,1:T(8,128)(2,1)}), bf16[8,512,1024]{2,0,1:T(8,128)(2,1)}, u32[]{:S(2)}, u32[]{:S(2)}) async-start(bf16[8,512,1024]{2,0,1:T(8,128)(2,1)} %copy.76), calls=%async_computation.1 | async-start | bytes 16777216 | tf_op jit(solution)/shard_map/all_to_all | solution.py:70
  801.3 179.8 %all-to-all-start.3 = ((bf16[8,512,1024]{2,0,1:T(8,128)(2,1)}), bf16[8,512,1024]{2,0,1:T(8,128)(2,1)}, u32[]{:S(2)}, u32[]{:S(2)}) async-start(bf16[8,512,1024]{2,0,1:T(8,128)(2,1)} %copy.79), calls=%async_computation.3 | async-start | bytes 16777216 | tf_op jit(solution)/shard_map/all_to_all | solution.py:73
  813.8 314.8 %reduce-scatter.2.cloned.1.call-start = ((), (), s32[]{:S(2)}) async-start(), calls=%async_computation.5 | async-start | bytes 6291456 | tf_op jit(solution)/shard_map/reduce_scatter | solution.py:104
Sparse Core Ops, SparseCore 0:
  1055.0 73.5 reduce-scatter.1
where the time goes:
time: 1150 us; the launch traced here: 1140 us
  waiting for transfers between devices  525 us (46%)
  blocking collectives  297 us (26%)
  local copies, waits for them, and re-layouts  151 us (13%)
  starting transfers between devices  56.3 us (5%)
  matrix products  49.8 us (4%)
  other arithmetic  44.7 us (4%)
  between operations  14.2 us (1%)
    all_gather x1, blocking collectives, body(): lists = lax.all_gather(key_blocks, 'seq', axis=0, tiled=True)  297 us
    ppermute x4, waiting for transfers between devices, partner(): lax.ppermute(value, axis, [(i, i ^ 1 << apart) for i in range(lax.axis_si...  201 us
    all_to_all x1, waiting for transfers between devices, body(): lax.all_to_all(send_v, 'seq', split_axis=1, concat_axis=1, tiled=True)  156 us
    all_to_all x1, waiting for transfers between devices, body(): lax.all_to_all(send_k, 'seq', split_axis=1, concat_axis=1, tiled=True)  79.2 us
    reduce_scatter x1, waiting for transfers between devices, body(): lax.psum_scatter(jnp.dot(attended, out_weight, preferred_element_type=jnp...  73.7 us
    reshape x2, local copies, waits for them, and re-layouts, body(): spread_k[chosen].reshape(slot_count, seq_count * slice_rows, feat_width)  24.2 us
    reshape x2, local copies, waits for them, and re-layouts, body(): spread_v[chosen].reshape(slot_count, seq_count * slice_rows, feat_width)  24 us
  transfers between devices with their start and end apart: 9, of which 8 were waited for; matrix products, arithmetic and copies ran while one was open for 11% of the time, Pallas kernels for 0%

commit v1 on v0

v1 whole, which is shorter than its diff:
```python
import functools
import math

import jax
import jax.numpy as jnp
from jax import lax
from jax.experimental import pallas as pl
from jax.experimental.pallas import tpu as pltpu
from jax.sharding import Mesh, PartitionSpec as P

TILE = 32
TCOLS = 8
HD = 128
SEL = 8
BLOCK = 512
PART = 128
SEQ = ("x", "zh", "zl", "yh", "yl")
LINE = ("zh", "zl")
PLANE = ("x", "yh", "yl")
BAND = ("zl", "yh", "yl")
SIZES = (4, 2, 4, 2, 2, 2)
CHUNKS = (1, 1, 1, 1)
VMEM_LIMIT = 48 * 1024 * 1024


def exchange(value, axes):
    return lax.all_to_all(value, axes, split_axis=0, concat_axis=0, tiled=True)


def picked(row, width):
    col = jnp.transpose(jnp.broadcast_to(row, (128, BLOCK)))
    lane = lax.broadcasted_iota(jnp.int32, (BLOCK, 128), 1)
    parts = [
        jnp.where(col == lane + 128 * k, 1.0, 0.0).astype(jnp.bfloat16) for k in range(width // 128)
    ]
    return jnp.concatenate(parts, axis=1)


def order_kv_kernel(place_ref, rows_ref, out_ref):
    tile = rows_ref[...].reshape(TILE * TILE, HD)
    for b in range(2):
        hot = picked(place_ref[0, b : b + 1, :], TILE * TILE)
        rows = jnp.dot(hot, tile, preferred_element_type=jnp.float32).astype(jnp.bfloat16)
        out_ref[:, b] = rows.reshape(4, PART, HD)


def order_kv(place, rows, tiles):
    return pl.pallas_call(
        order_kv_kernel,
        grid=(tiles,),
        in_specs=[
            pl.BlockSpec((1, 2, BLOCK), lambda t: (t, 0, 0)),
            pl.BlockSpec((TILE, 1, TILE, HD), lambda t: (0, t, 0, 0)),
        ],
        out_specs=pl.BlockSpec((4, 2, PART, HD), lambda t: (0, t, 0, 0)),
        out_shape=jax.ShapeDtypeStruct((4, 2 * tiles, PART, HD), jnp.bfloat16),
        compiler_params=pltpu.CompilerParams(vmem_limit_bytes=VMEM_LIMIT),
        cost_estimate=pl.CostEstimate(
            flops=tiles * 4 * BLOCK * TILE * TILE * HD, bytes_accessed=tiles * 2**19, transcendentals=0
        ),
        name="order_kv",
    )(place, rows)


def order_q_kernel(place_ref, near_ref, far_ref, out_ref):
    hot = picked(place_ref[...], 2 * BLOCK)
    rows = jnp.dot(hot[:, :BLOCK], near_ref[...], preferred_element_type=jnp.float32)
    rows += jnp.dot(hot[:, BLOCK:], far_ref[...], preferred_element_type=jnp.float32)
    out_ref[...] = rows.astype(jnp.bfloat16)


def order_q(place, near, far):
    width = near.shape[1]
    return pl.pallas_call(
        order_q_kernel,
        grid=(2,),
        in_specs=[
            pl.BlockSpec((1, BLOCK), lambda t: (0, 0)),
            pl.BlockSpec((BLOCK, width // 2), lambda t: (0, t)),
            pl.BlockSpec((BLOCK, width // 2), lambda t: (0, t)),
        ],
        out_specs=pl.BlockSpec((BLOCK, width // 2), lambda t: (0, t)),
        out_shape=jax.ShapeDtypeStruct((BLOCK, width), jnp.bfloat16),
        compiler_params=pltpu.CompilerParams(vmem_limit_bytes=VMEM_LIMIT),
        cost_estimate=pl.CostEstimate(
            flops=4 * BLOCK * BLOCK * width, bytes_accessed=3 * 2**20, transcendentals=0
        ),
        name="order_q",
    )(place, near, far)


def select_kernel(blocks_ref, held_ref, out_ref, sem, *, per_group):
    def send(step, carry):
        reader = step // SEL
        slot = step % SEL
        block = blocks_ref[reader, slot]
        col = lax.shift_right_logical(block, 5)
        half = lax.shift_right_logical(block, 4) & 1
        group = (block & 15) // per_group
        place = (block & 15) % per_group
        pltpu.make_async_copy(
            held_ref.at[half, :, group, col, place], out_ref.at[reader, :, slot], sem
        ).start()
        return carry

    lax.fori_loop(0, 16 * SEL, send, 0)
    pltpu.make_async_copy(out_ref, out_ref, sem).wait()


def select(blocks, held):
    half, slabs, groups, cols, per_group = held.shape[:5]
    return pl.pallas_call(
        functools.partial(select_kernel, per_group=per_group),
        grid_spec=pltpu.PrefetchScalarGridSpec(
            num_scalar_prefetch=1,
            grid=(1,),
            in_specs=[pl.BlockSpec(memory_space=pl.ANY)],
            out_specs=pl.BlockSpec((16, slabs, SEL, PART, HD), lambda g, blocks: (0, 0, 0, 0, 0)),
            scratch_shapes=[pltpu.SemaphoreType.DMA],
        ),
        out_shape=jax.ShapeDtypeStruct((16, slabs, SEL, PART, HD), jnp.bfloat16),
        compiler_params=pltpu.CompilerParams(vmem_limit_bytes=VMEM_LIMIT),
        cost_estimate=pl.CostEstimate(
            flops=0, bytes_accessed=slabs * 2**23, transcendentals=0
        ),
        name="select",
    )(blocks, held)


def attend_kernel(q_ref, k_ref, v_ref, out_ref, *, scale):
    sub = BLOCK // 2
    for r in range(2):
        query = q_ref[r * sub : (r + 1) * sub, :]
        top = jnp.full((sub, 1), -jnp.inf, jnp.float32)
        total = jnp.zeros((sub, 1), jnp.float32)
        mixed = jnp.zeros((sub, HD), jnp.float32)
        for c in range(4):
            keys = k_ref[c, 0, 0, 0]
            values = v_ref[c, 0, 0, 0]
            scores = lax.dot_general(
                query, keys, (((1,), (1,)), ((), ())), preferred_element_type=jnp.float32
            )
            peak = jnp.maximum(top, jnp.max(scores, axis=1, keepdims=True))
            weights = jnp.exp2(scores * scale - peak * scale)
            fade = jnp.exp2((top - peak) * scale)
            total = total * fade + jnp.sum(weights, axis=1, keepdims=True)
            mixed = mixed * fade + jnp.dot(
                weights.astype(jnp.bfloat16), values, preferred_element_type=jnp.float32
            )
            top = peak
        out_ref[r * sub : (r + 1) * sub, :] = (mixed / total).astype(jnp.bfloat16)


def attend(query, fetched, first, slabs):
    rows = SEL * PART
    spec = (4, 1, 1, 1, rows, HD)
    heads = 2 * slabs
    return pl.pallas_call(
        functools.partial(attend_kernel, scale=math.log2(math.e) / math.sqrt(HD)),
        grid=(heads,),
        in_specs=[
            pl.BlockSpec((BLOCK, HD), lambda g: (0, first + g)),
            pl.BlockSpec(spec, lambda g: (0, g % 2, 0, g // 2, 0, 0)),
            pl.BlockSpec(spec, lambda g: (0, g % 2, 1, g // 2, 0, 0)),
        ],
        out_specs=pl.BlockSpec((BLOCK, HD), lambda g: (0, g)),
        out_shape=jax.ShapeDtypeStruct((BLOCK, heads * HD), jnp.bfloat16),
        compiler_params=pltpu.CompilerParams(vmem_limit_bytes=VMEM_LIMIT),
        cost_estimate=pl.CostEstimate(
            flops=heads * 4 * BLOCK * 4 * rows * HD * 4,
            bytes_accessed=heads * 2**21,
            transcendentals=heads * BLOCK * 4 * rows,
        ),
        name="attend",
    )(query, fetched, fetched)


def body(q_raster, k_raster, v_raster, hilbert_order, key_blocks, out_weight):
    width = q_raster.shape[1]
    image_width = TILE * TCOLS
    core = lax.axis_index("core")
    swap = [(0, 1), (1, 0)]
    weight_far = lax.ppermute(out_weight, "core", swap)

    in_tile = hilbert_order // image_width % TILE * TILE + hilbert_order % image_width % TILE
    band_places = exchange(jnp.broadcast_to(in_tile[None, None], (16, 1, BLOCK)), BAND)
    lists = exchange(jnp.broadcast_to(key_blocks[None], (16, 1, SEL)), PLANE).reshape(16, SEL)

    key_lines = k_raster.reshape(2, TCOLS, TILE, width // HD, HD)
    value_lines = v_raster.reshape(2, TCOLS, TILE, width // HD, HD)
    both = jnp.stack([key_lines, value_lines])
    line_pos = lax.axis_index("zl")

    fetched = []
    first = 0
    for slabs in CHUNKS:
        groups = 4 // slabs
        tiles = TCOLS // groups
        part = lax.slice_in_dim(both, first, first + 2 * slabs, axis=4)
        part = part.reshape(2, 2, groups, tiles, TILE, slabs, 2, HD)
        part = jnp.transpose(part, (5, 2, 6, 0, 1, 3, 4, 7)).reshape(16, 2, tiles, TILE, HD)
        rows = exchange(part, BAND).reshape(TILE, tiles, TILE, HD)
        group = line_pos % groups
        place = lax.dynamic_slice_in_dim(
            band_places.reshape(TCOLS, 2, BLOCK), group * tiles, tiles, axis=0
        )
        ordered = order_kv(place, rows, tiles)
        spread = exchange(ordered, "x")
        held = lax.all_gather(spread, LINE, axis=0)
        held = held.reshape(2, slabs, groups, 4, 2 * tiles, PART, HD)
        sent = select(lists, held)
        got = exchange(sent, PLANE)
        fetched.append((first, slabs, got.reshape(4, 2, 2, slabs, SEL * PART, HD)))
        first += 2 * slabs

    lines = q_raster.reshape(2, TCOLS, TILE, width)
    toward = jnp.transpose(lines, (1, 0, 2, 3))
    near = exchange(toward, ("zl", "yh")).reshape(BLOCK, width)
    far = lax.ppermute(near, "yl", swap)
    line = in_tile // TILE
    from_yl = line // 2 % 2
    q_place = (
        jnp.where(from_yl == lax.axis_index("yl"), 0, BLOCK)
        + (line // 8 * 2 + line // 4 % 2) * 64
        + line % 2 * TILE
        + in_tile % TILE
    )
    query = order_q(q_place[None], near, far)

    half = BLOCK // 2
    result = jnp.zeros((half, out_weight.shape[1]), jnp.float32)
    for first, slabs, got in fetched:
        attended = attend(query, got, first, slabs)
        mine = lax.dynamic_slice_in_dim(attended, core * half, half, axis=0)
        theirs = lax.dynamic_slice_in_dim(attended, (1 - core) * half, half, axis=0)
        other = lax.ppermute(theirs, "core", swap)
        feats = slice(first * HD, (first + 2 * slabs) * HD)
        result += jnp.dot(mine, out_weight[feats], preferred_element_type=jnp.float32)
        result += jnp.dot(other, weight_far[feats], preferred_element_type=jnp.float32)
    return result.astype(jnp.bfloat16)


def solution(mesh):
    split = Mesh(mesh.devices.reshape(SIZES), SEQ + ("core",))
    placed = (
        P(SEQ, "core"),
        P(SEQ, "core"),
        P(SEQ, "core"),
        P(SEQ),
        P(SEQ, None),
        P("core", None),
    )
    return jax.shard_map(
        body, mesh=split, in_specs=placed, out_specs=P(SEQ + ("core",), None), check_vma=False
    )
```

time: 1150 us -> 486 us (0.42)
  the two profiles are of different devices: /device:TPU:1 before, /device:TPU:115 now
where the time goes in v1:
time: 486 us; the launch traced here: 484 us
  waiting for transfers between devices  185 us (38%)
  starting transfers between devices  123 us (25%)
  Pallas kernels  65.5 us (13%)
  blocking collectives  62.8 us (13%)
  local copies, waits for them, and re-layouts  17.5 us (4%)
  matrix products  15.6 us (3%)
  between operations  13.5 us (3%)
    all_to_all x11, waiting for transfers between devices, exchange(): return lax.all_to_all(value, axes, split_axis=0, concat_axis=0, tiled=True)  150 us
    all_to_all x11, starting transfers between devices, exchange(): return lax.all_to_all(value, axes, split_axis=0, concat_axis=0, tiled=True)  82.5 us
    all_to_all x4, blocking collectives, exchange(): return lax.all_to_all(value, axes, split_axis=0, concat_axis=0, tiled=True)  62.8 us
    pallas_call x4, Pallas kernels, attend(): pl.pallas_call(functools.partial(attend_kernel, scale=math.log2(math.e) /...  39.7 us
    ppermute x4, starting transfers between devices, body(): other = lax.ppermute(theirs, 'core', swap)  30.5 us
    all_gather x4, waiting for transfers between devices, body(): held = lax.all_gather(spread, LINE, axis=0)  17.7 us
    pallas_call x4, Pallas kernels, select(): pl.pallas_call(functools.partial(select_kernel, per_group=per_group), gri...  16.3 us
    ppermute x1, waiting for transfers between devices, body(): far = lax.ppermute(near, 'yl', swap)  16.1 us
  transfers between devices with their start and end apart: 21, of which 12 were waited for; matrix products, arithmetic and copies ran while one was open for 4% of the time, Pallas kernels for 13%

profile of v1, /device:TPU:115, one launch (start us, length us, event | category | flops | bytes accessed | tf_op | source)
XLA Modules:
  0.0 484.4 jit_solution(1414058022541014179)
XLA Ops:
  7.9 7.0 %all-to-all-start.2 = ((s32[16,1,512]{2,1,0:T(1,128)}), s32[16,1,512]{2,1,0:T(1,128)S(1)}, u32[]{:S(2)}, u32[]{:S(2)}) async-start(s32[16,1,512]{2,1,0:T(1,128)} %broadcast_in_dim.27), calls=%async_computation.2 | async-start | bytes 65536 | tf_op jit(solution)/shard_map/all_to_all | solution.py:27
  19.7 7.0 %all-to-all-start.6 = ((bf16[16,2,2,32,128]{4,3,2,1,0:T(8,128)(2,1)}), bf16[16,2,2,32,128]{4,3,2,1,0:T(8,128)(2,1)S(1)}, u32[]{:S(2)}, u32[]{:S(2)}) async-start(bf16[16,2,2,32,128]{4,3,2,1,0:T(8,128)(2,1)} %bitcast.16), calls=%async_computation.6 | async-start | bytes 1048576 | tf_op jit(solution)/shard_map/all_to_all | solution.py:27
  26.9 11.7 %all-to-all-done.6 = bf16[16,2,2,32,128]{4,3,2,1,0:T(8,128)(2,1)S(1)} async-done(((bf16[16,2,2,32,128]{4,3,2,1,0:T(8,128)(2,1)}), bf16[16,2,2,32,128]{4,3,2,1,0:T(8,128)(2,1)S(1)}, u32[]{:S(2)}, u32[]{:S(2)}) %all-to-all-start.6) | async-done | bytes 524320 | tf_op jit(solution)/shard_map/all_to_all | solution.py:27
  40.2 10.2 %all_to_all.75 = bf16[4,4,128,128]{3,2,1,0:T(8,128)(2,1)} all-to-all(bf16[4,4,128,128]{3,2,1,0:T(8,128)(2,1)S(1)} %order_kv.5), channel_id=1, replica_groups=mesh['x'=4,'zh'=2,'zl'=4,'yh'=2,'yl'=2,'core'=2] {'x'}, dimensions={0} | all-to-all | bytes 1048576 | tf_op jit(solution)/shard_map/all_to_all | solution.py:27
  50.7 19.5 %all_to_all.76 = bf16[16,2,2,32,128]{4,3,2,1,0:T(8,128)(2,1)S(1)} all-to-all(bf16[16,2,2,32,128]{4,3,2,1,0:T(8,128)(2,1)S(1)} %bitcast.69), channel_id=1, replica_groups=mesh['x'=4,'zh'=2,'zl'=4,'yh'=2,'yl'=2,'core'=2] {'zl','yh','yl'}, dimensions={0} | all-to-all | bytes 1048576 | tf_op jit(solution)/shard_map/all_to_all | solution.py:27
  71.8 10.5 %all_to_all.77 = bf16[4,4,128,128]{3,2,1,0:T(8,128)(2,1)} all-to-all(bf16[4,4,128,128]{3,2,1,0:T(8,128)(2,1)S(1)} %order_kv.4), channel_id=1, replica_groups=mesh['x'=4,'zh'=2,'zl'=4,'yh'=2,'yl'=2,'core'=2] {'x'}, dimensions={0} | all-to-all | bytes 1048576 | tf_op jit(solution)/shard_map/all_to_all | solution.py:27
  82.4 22.6 %all_to_all.78 = bf16[16,2,2,32,128]{4,3,2,1,0:T(8,128)(2,1)S(1)} all-to-all(bf16[16,2,2,32,128]{4,3,2,1,0:T(8,128)(2,1)S(1)} %bitcast.70), channel_id=1, replica_groups=mesh['x'=4,'zh'=2,'zl'=4,'yh'=2,'yl'=2,'core'=2] {'zl','yh','yl'}, dimensions={0} | all-to-all | bytes 1048576 | tf_op jit(solution)/shard_map/all_to_all | solution.py:27
  117.8 8.9 %all-to-all-start.12 = ((bf16[16,2,2,32,128]{4,3,2,1,0:T(8,128)(2,1)}), bf16[16,2,2,32,128]{4,3,2,1,0:T(8,128)(2,1)S(1)}, u32[]{:S(2)}, u32[]{:S(2)}) async-start(bf16[16,2,2,32,128]{4,3,2,1,0:T(8,128)(2,1)} %bitcast.30), calls=%async_computation.12 | async-start | bytes 1048576 | tf_op jit(solution)/shard_map/all_to_all | solution.py:27
  154.6 7.9 %all-to-all-start = ((bf16[8,2,32,1024]{3,2,1,0:T(8,128)(2,1)}), bf16[8,2,32,1024]{3,2,1,0:T(8,128)(2,1)S(1)}, u32[]{:S(2)}, u32[]{:S(2)}) async-start(bf16[8,2,32,1024]{3,2,1,0:T(8,128)(2,1)} %bitcast.51), calls=%async_computation | async-start | bytes 2097152 | tf_op jit(solution)/shard_map/all_to_all | solution.py:27
  168.5 20.0 %all-to-all-done = bf16[8,2,32,1024]{3,2,1,0:T(8,128)(2,1)S(1)} async-done(((bf16[8,2,32,1024]{3,2,1,0:T(8,128)(2,1)}), bf16[8,2,32,1024]{3,2,1,0:T(8,128)(2,1)S(1)}, u32[]{:S(2)}, u32[]{:S(2)}) %all-to-all-start) | async-done | bytes 1048608 | tf_op jit(solution)/shard_map/all_to_all | solution.py:27
  201.2 43.2 %all-to-all-done.8 = bf16[16,1,8,128,128]{4,3,2,1,0:T(8,128)(2,1)} async-done(((bf16[16,1,8,128,128]{4,3,2,1,0:T(8,128)(2,1)}), bf16[16,1,8,128,128]{4,3,2,1,0:T(8,128)(2,1)}, u32[]{:S(2)}, u32[]{:S(2)}) %all-to-all-start.8) | async-done | bytes 4194336 | tf_op jit(solution)/shard_map/all_to_all | solution.py:27
  244.4 7.0 %all-to-all-start.5 = ((bf16[16,1,8,128,128]{4,3,2,1,0:T(8,128)(2,1)}), bf16[16,1,8,128,128]{4,3,2,1,0:T(8,128)(2,1)}, u32[]{:S(2)}, u32[]{:S(2)}) async-start(bf16[16,1,8,128,128]{4,3,2,1,0:T(8,128)(2,1)} %copy-done.1), calls=%async_computation.5 | async-start | bytes 8388608 | tf_op jit(solution)/shard_map/all_to_all | solution.py:27
  264.2 32.2 %all-to-all-done.5 = bf16[16,1,8,128,128]{4,3,2,1,0:T(8,128)(2,1)} async-done(((bf16[16,1,8,128,128]{4,3,2,1,0:T(8,128)(2,1)}), bf16[16,1,8,128,128]{4,3,2,1,0:T(8,128)(2,1)}, u32[]{:S(2)}, u32[]{:S(2)}) %all-to-all-start.5) | async-done | bytes 4194336 | tf_op jit(solution)/shard_map/all_to_all | solution.py:27
  296.5 11.9 %all-to-all-start.11 = ((bf16[16,1,8,128,128]{4,3,2,1,0:T(8,128)(2,1)}), bf16[16,1,8,128,128]{4,3,2,1,0:T(8,128)(2,1)}, u32[]{:S(2)}, u32[]{:S(2)}) async-start(bf16[16,1,8,128,128]{4,3,2,1,0:T(8,128)(2,1)} %copy-done.2), calls=%async_computation.11 | async-start | bytes 8388608 | tf_op jit(solution)/shard_map/all_to_all | solution.py:27
  309.3 11.6 %all-gather.15.cloned.1.call-done = bf16[32,4,128,128]{3,2,1,0:T(8,128)(2,1)} async-done(((bf16[4,4,128,128]{3,2,1,0:T(8,128)(2,1)}), bf16[32,4,128,128]{3,2,1,0:T(8,128)(2,1)}) %all-gather.15.cloned.1.call-update) | async-done | bytes 4194320 | tf_op jit(solution)/shard_map/all_gather | solution.py:209
  326.8 26.3 %all-to-all-done.11 = bf16[16,1,8,128,128]{4,3,2,1,0:T(8,128)(2,1)} async-done(((bf16[16,1,8,128,128]{4,3,2,1,0:T(8,128)(2,1)}), bf16[16,1,8,128,128]{4,3,2,1,0:T(8,128)(2,1)}, u32[]{:S(2)}, u32[]{:S(2)}) %all-to-all-start.11) | async-done | bytes 4194336 | tf_op jit(solution)/shard_map/all_to_all | solution.py:27
  353.1 11.4 %all-to-all-start.14 = ((bf16[16,1,8,128,128]{4,3,2,1,0:T(8,128)(2,1)}), bf16[16,1,8,128,128]{4,3,2,1,0:T(8,128)(2,1)}, u32[]{:S(2)}, u32[]{:S(2)}) async-start(bf16[16,1,8,128,128]{4,3,2,1,0:T(8,128)(2,1)} %copy-done), calls=%async_computation.14 | async-start | bytes 8388608 | tf_op jit(solution)/shard_map/all_to_all | solution.py:27
  364.5 9.4 %collective-permute-start.2 = (bf16[1024,2048]{1,0:T(8,128)(2,1)}, bf16[1024,2048]{1,0:T(8,128)(2,1)}, u32[]{:S(2)}, u32[]{:S(2)}) collective-permute-start(bf16[1024,2048]{1,0:T(8,128)(2,1)} %param.11), channel_id=1, source_target_pairs={{0,1},{1,0},{2,3},{3,2},{4,5},{5,4},{6,7},{7,6},{8,9},{9,8},{10,11... | collective-permute-start | bytes 12582920 | tf_op jit(solution)/shard_map/ppermute | solution.py:183
  373.9 16.1 %collective-permute-done.far_ref = bf16[512,1024]{1,0:T(8,128)(2,1)S(1)} collective-permute-done((bf16[512,1024]{1,0:T(8,128)(2,1)S(1)}, bf16[512,1024]{1,0:T(8,128)(2,1)S(1)}, u32[]{:S(2)}, u32[]{:S(2)}) %collective-permute-start) | collective-permute-done | bytes 1048608 | tf_op jit(solution)/shard_map/ppermute | solution.py:219
  391.8 9.9 %attend.5 = bf16[512,256]{1,0:T(8,128)(2,1)S(1)} custom-call(bf16[512,1024]{1,0:T(8,128)(2,1)S(1)} %order_q.1.q_ref, bf16[4,2,2,1,1024,128]{5,4,3,2,1,0:T(8,128)(2,1)} %bitcast.19.k_ref.v_ref, bf16[4,2,2,1,1024,128]{5,4,3,2,1,0:T(8,128)(2,1)} %bitcast.19.k_ref.v_ref), custom_call_target="tpu_custom_call" | custom-call | flops 8589934592 | bytes 4194304 | tf_op jit(solution)/shard_map/attend/pallas_call | solution.py:158
  401.7 29.2 %collective-permute-start.3 = (bf16[256,256]{1,0:T(8,128)(2,1)S(1)}, bf16[256,256]{1,0:T(8,128)(2,1)S(1)}, u32[]{:S(2)}, u32[]{:S(2)}) collective-permute-start(bf16[256,256]{1,0:T(8,128)(2,1)S(1)} %constant_dynamic-slice_fusion.2), channel_id=1, source_target_pairs={{0,1},{1,0},{2,3},{3,2},{4,5},{5,4},{6,7},{7,6},{8,9},{9,8},{10,11... | collective-permute-start | bytes 393224 | tf_op jit(solution)/shard_map/ppermute | solution.py:236
  430.9 9.9 %attend.4 = bf16[512,256]{1,0:T(8,128)(2,1)S(1)} custom-call(bf16[512,1024]{1,0:T(8,128)(2,1)S(1)} %order_q.1.q_ref, bf16[4,2,2,1,1024,128]{5,4,3,2,1,0:T(8,128)(2,1)} %bitcast.12.k_ref.v_ref, bf16[4,2,2,1,1024,128]{5,4,3,2,1,0:T(8,128)(2,1)} %bitcast.12.k_ref.v_ref), custom_call_target="tpu_custom_call" | custom-call | flops 8589934592 | bytes 4194304 | tf_op jit(solution)/shard_map/attend/pallas_call | solution.py:158
  441.1 10.0 %attend.6 = bf16[512,256]{1,0:T(8,128)(2,1)S(1)} custom-call(bf16[512,1024]{1,0:T(8,128)(2,1)S(1)} %order_q.1.q_ref, bf16[4,2,2,1,1024,128]{5,4,3,2,1,0:T(8,128)(2,1)} %bitcast.26.k_ref.v_ref, bf16[4,2,2,1,1024,128]{5,4,3,2,1,0:T(8,128)(2,1)} %bitcast.26.k_ref.v_ref), custom_call_target="tpu_custom_call" | custom-call | flops 8589934592 | bytes 4194304 | tf_op jit(solution)/shard_map/attend/pallas_call | solution.py:158
  455.3 9.9 %attend.7 = bf16[512,256]{1,0:T(8,128)(2,1)S(1)} custom-call(bf16[512,1024]{1,0:T(8,128)(2,1)S(1)} %order_q.1.q_ref, bf16[4,2,2,1,1024,128]{5,4,3,2,1,0:T(8,128)(2,1)} %bitcast.33.k_ref.v_ref, bf16[4,2,2,1,1024,128]{5,4,3,2,1,0:T(8,128)(2,1)} %bitcast.33.k_ref.v_ref), custom_call_target="tpu_custom_call" | custom-call | flops 8589934592 | bytes 4194304 | tf_op jit(solution)/shard_map/attend/pallas_call | solution.py:158
  (89 shorter events, 107.6 us)
Async XLA Ops:
  7.9 11.8 %all-to-all-start.2 = ((s32[16,1,512]{2,1,0:T(1,128)}), s32[16,1,512]{2,1,0:T(1,128)S(1)}, u32[]{:S(2)}, u32[]{:S(2)}) async-start(s32[16,1,512]{2,1,0:T(1,128)} %broadcast_in_dim.27), calls=%async_computation.2 | async-start | bytes 65536 | tf_op jit(solution)/shard_map/all_to_all | solution.py:27
  19.7 18.9 %all-to-all-start.6 = ((bf16[16,2,2,32,128]{4,3,2,1,0:T(8,128)(2,1)}), bf16[16,2,2,32,128]{4,3,2,1,0:T(8,128)(2,1)S(1)}, u32[]{:S(2)}, u32[]{:S(2)}) async-start(bf16[16,2,2,32,128]{4,3,2,1,0:T(8,128)(2,1)} %bitcast.16), calls=%async_computation.6 | async-start | bytes 1048576 | tf_op jit(solution)/shard_map/all_to_all | solution.py:27
  26.7 135.8 %all-gather.11.cloned.1.call-start = ((), (), s32[]{:S(2)}) async-start(), calls=%async_computation.16 | async-start | bytes 4718592 | tf_op jit(solution)/shard_map/all_gather | solution.py:209
  50.5 144.6 %all-gather.9.cloned.1.call-start = ((), (), s32[]{:S(2)}) async-start(), calls=%async_computation.15 | async-start | bytes 4718592 | tf_op jit(solution)/shard_map/all_gather | solution.py:209
  107.3 26.7 %copy-start.10 = (s32[1,8]{1,0:T(1,128)S(1)}, s32[1,8]{1,0:T(1,128)}, u32[]{:S(2)}) copy-start(s32[1,8]{1,0:T(1,128)} %param.10) | copy-start | bytes 100
  107.3 10.5 %all-to-all-start.10 = ((bf16[4,4,128,128]{3,2,1,0:T(8,128)(2,1)}), bf16[4,4,128,128]{3,2,1,0:T(8,128)(2,1)S(1)}, u32[]{:S(2)}, u32[]{:S(2)}) async-start(bf16[4,4,128,128]{3,2,1,0:T(8,128)(2,1)} %order_kv.6), calls=%async_computation.10 | async-start | bytes 1048576 | tf_op jit(solution)/shard_map/all_to_all | solution.py:27
  117.8 16.2 %all-to-all-start.12 = ((bf16[16,2,2,32,128]{4,3,2,1,0:T(8,128)(2,1)}), bf16[16,2,2,32,128]{4,3,2,1,0:T(8,128)(2,1)S(1)}, u32[]{:S(2)}, u32[]{:S(2)}) async-start(bf16[16,2,2,32,128]{4,3,2,1,0:T(8,128)(2,1)} %bitcast.30), calls=%async_computation.12 | async-start | bytes 1048576 | tf_op jit(solution)/shard_map/all_to_all | solution.py:27
  126.7 131.4 %all-gather.13.cloned.1.call-start = ((), (), s32[]{:S(2)}) async-start(), calls=%async_computation.17 | async-start | bytes 4718592 | tf_op jit(solution)/shard_map/all_gather | solution.py:209
  134.6 9.5 %all-to-all-start.1 = ((s32[16,1,8]{2,1,0:T(1,128)}), s32[16,1,8]{2,1,0:T(1,128)S(1)}, u32[]{:S(2)}, u32[]{:S(2)}) async-start(s32[16,1,8]{2,1,0:T(1,128)} %broadcast_in_dim.26), calls=%async_computation.1 | async-start | bytes 16384 | tf_op jit(solution)/shard_map/all_to_all | solution.py:27
  144.1 10.5 %all-to-all-start.13 = ((bf16[4,4,128,128]{3,2,1,0:T(8,128)(2,1)}), bf16[4,4,128,128]{3,2,1,0:T(8,128)(2,1)S(1)}, u32[]{:S(2)}, u32[]{:S(2)}) async-start(bf16[4,4,128,128]{3,2,1,0:T(8,128)(2,1)} %order_kv.7), calls=%async_computation.13 | async-start | bytes 1048576 | tf_op jit(solution)/shard_map/all_to_all | solution.py:27
  154.6 12.0 %copy-start.8 = (bf16[4,4,128,128]{3,2,1,0:T(8,128)(2,1)}, bf16[4,4,128,128]{3,2,1,0:T(8,128)(2,1)S(1)}, u32[]{:S(2)}) copy-start(bf16[4,4,128,128]{3,2,1,0:T(8,128)(2,1)S(1)} %all-to-all-done.13) | copy-start | bytes 1572868
  154.6 33.9 %all-to-all-start = ((bf16[8,2,32,1024]{3,2,1,0:T(8,128)(2,1)}), bf16[8,2,32,1024]{3,2,1,0:T(8,128)(2,1)S(1)}, u32[]{:S(2)}, u32[]{:S(2)}) async-start(bf16[8,2,32,1024]{3,2,1,0:T(8,128)(2,1)} %bitcast.51), calls=%async_computation | async-start | bytes 2097152 | tf_op jit(solution)/shard_map/all_to_all | solution.py:27
  188.5 55.9 %all-to-all-start.8 = ((bf16[16,1,8,128,128]{4,3,2,1,0:T(8,128)(2,1)}), bf16[16,1,8,128,128]{4,3,2,1,0:T(8,128)(2,1)}, u32[]{:S(2)}, u32[]{:S(2)}) async-start(bf16[16,1,8,128,128]{4,3,2,1,0:T(8,128)(2,1)} %copy-done.3), calls=%async_computation.8 | async-start | bytes 8388608 | tf_op jit(solution)/shard_map/all_to_all | solution.py:27
  244.4 52.0 %all-to-all-start.5 = ((bf16[16,1,8,128,128]{4,3,2,1,0:T(8,128)(2,1)}), bf16[16,1,8,128,128]{4,3,2,1,0:T(8,128)(2,1)}, u32[]{:S(2)}, u32[]{:S(2)}) async-start(bf16[16,1,8,128,128]{4,3,2,1,0:T(8,128)(2,1)} %copy-done.1), calls=%async_computation.5 | async-start | bytes 8388608 | tf_op jit(solution)/shard_map/all_to_all | solution.py:27
  251.4 69.4 %all-gather.15.cloned.1.call-start = ((), (), s32[]{:S(2)}) async-start(), calls=%async_computation.18 | async-start | bytes 4718592 | tf_op jit(solution)/shard_map/all_gather | solution.py:209
  296.5 56.7 %all-to-all-start.11 = ((bf16[16,1,8,128,128]{4,3,2,1,0:T(8,128)(2,1)}), bf16[16,1,8,128,128]{4,3,2,1,0:T(8,128)(2,1)}, u32[]{:S(2)}, u32[]{:S(2)}) async-start(bf16[16,1,8,128,128]{4,3,2,1,0:T(8,128)(2,1)} %copy-done.2), calls=%async_computation.11 | async-start | bytes 8388608 | tf_op jit(solution)/shard_map/all_to_all | solution.py:27
  308.4 81.7 %collective-permute-start = (bf16[512,1024]{1,0:T(8,128)(2,1)S(1)}, bf16[512,1024]{1,0:T(8,128)(2,1)S(1)}, u32[]{:S(2)}, u32[]{:S(2)}) collective-permute-start(bf16[512,1024]{1,0:T(8,128)(2,1)S(1)} %bitcast.52), channel_id=1, source_target_pairs={{0,2},{2,0},{1,3},{3,1},{4,6},{6,4},{5,7},{7,5},{8,10},{10,8},{9,1... | collective-permute-start | bytes 3145736 | tf_op jit(solution)/shard_map/ppermute | solution.py:219
  353.1 102.2 %all-to-all-start.14 = ((bf16[16,1,8,128,128]{4,3,2,1,0:T(8,128)(2,1)}), bf16[16,1,8,128,128]{4,3,2,1,0:T(8,128)(2,1)}, u32[]{:S(2)}, u32[]{:S(2)}) async-start(bf16[16,1,8,128,128]{4,3,2,1,0:T(8,128)(2,1)} %copy-done), calls=%async_computation.14 | async-start | bytes 8388608 | tf_op jit(solution)/shard_map/all_to_all | solution.py:27
  364.5 102.8 %collective-permute-start.2 = (bf16[1024,2048]{1,0:T(8,128)(2,1)}, bf16[1024,2048]{1,0:T(8,128)(2,1)}, u32[]{:S(2)}, u32[]{:S(2)}) collective-permute-start(bf16[1024,2048]{1,0:T(8,128)(2,1)} %param.11), channel_id=1, source_target_pairs={{0,1},{1,0},{2,3},{3,2},{4,5},{5,4},{6,7},{7,6},{8,9},{9,8},{10,11... | collective-permute-start | bytes 12582920 | tf_op jit(solution)/shard_map/ppermute | solution.py:183
  401.7 65.6 %collective-permute-start.3 = (bf16[256,256]{1,0:T(8,128)(2,1)S(1)}, bf16[256,256]{1,0:T(8,128)(2,1)S(1)}, u32[]{:S(2)}, u32[]{:S(2)}) collective-permute-start(bf16[256,256]{1,0:T(8,128)(2,1)S(1)} %constant_dynamic-slice_fusion.2), channel_id=1, source_target_pairs={{0,1},{1,0},{2,3},{3,2},{4,5},{5,4},{6,7},{7,6},{8,9},{9,8},{10,11... | collective-permute-start | bytes 393224 | tf_op jit(solution)/shard_map/ppermute | solution.py:236
  440.8 28.2 %collective-permute-start.1 = (bf16[256,256]{1,0:T(8,128)(2,1)S(1)}, bf16[256,256]{1,0:T(8,128)(2,1)S(1)}, u32[]{:S(2)}, u32[]{:S(2)}) collective-permute-start(bf16[256,256]{1,0:T(8,128)(2,1)S(1)} %constant_dynamic-slice_fusion.3), channel_id=1, source_target_pairs={{0,1},{1,0},{2,3},{3,2},{4,5},{5,4},{6,7},{7,6},{8,9},{9,8},{10,11... | collective-permute-start | bytes 393224 | tf_op jit(solution)/shard_map/ppermute | solution.py:236
  441.1 10.6 %copy-start.6 = (bf16[1024,2048]{1,0:T(8,128)(2,1)S(1)}, bf16[1024,2048]{1,0:T(8,128)(2,1)}, u32[]{:S(2)}) copy-start(bf16[1024,2048]{1,0:T(8,128)(2,1)} %param.11) | copy-start | bytes 12582916
  451.2 19.4 %collective-permute-start.4 = (bf16[256,256]{1,0:T(8,128)(2,1)S(1)}, bf16[256,256]{1,0:T(8,128)(2,1)S(1)}, u32[]{:S(2)}, u32[]{:S(2)}) collective-permute-start(bf16[256,256]{1,0:T(8,128)(2,1)S(1)} %constant_dynamic-slice_fusion.1), channel_id=1, source_target_pairs={{0,1},{1,0},{2,3},{3,2},{4,5},{5,4},{6,7},{7,6},{8,9},{9,8},{10,11... | collective-permute-start | bytes 393224 | tf_op jit(solution)/shard_map/ppermute | solution.py:236
  466.9 5.6 %collective-permute-start.5 = (bf16[256,256]{1,0:T(8,128)(2,1)S(1)}, bf16[256,256]{1,0:T(8,128)(2,1)S(1)}, u32[]{:S(2)}, u32[]{:S(2)}) collective-permute-start(bf16[256,256]{1,0:T(8,128)(2,1)S(1)} %constant_dynamic-slice_fusion), channel_id=1, source_target_pairs={{0,1},{1,0},{2,3},{3,2},{4,5},{5,4},{6,7},{7,6},{8,9},{9,8},{10,11... | collective-permute-start | bytes 393224 | tf_op jit(solution)/shard_map/ppermute | solution.py:236
  (8 other events, 24.0 us)
Sparse Core Ops, SparseCore 0:
  50.6 68.4 all-gather.10
  120.9 68.8 all-gather.8
  191.6 66.4 all-gather.12
  259.8 60.9 all-gather.14

commit v2 on v1

v2 whole, which is shorter than its diff:
```python
import functools
import itertools
import math

import jax
import jax.numpy as jnp
from jax import lax
from jax.experimental import pallas as pl
from jax.experimental.pallas import tpu as pltpu
from jax.sharding import Mesh, PartitionSpec as P

TILE = 32
TCOLS = 8
HD = 128
SEL = 8
BLOCK = 512
PART = 128
SEQ = ("x", "zh", "zl", "yh", "yl")
LINE = ("zh", "zl")
PLANE = ("x", "yh", "yl")
BAND = ("zl", "yh", "yl")
SIZES = (4, 2, 4, 2, 2, 2)
CHUNKS = 4
LEAD = 1
TILES = 2
VMEM_LIMIT = 48 * 1024 * 1024


def exchange(value, axes):
    return lax.all_to_all(value, axes, split_axis=0, concat_axis=0, tiled=True)


def after(value, *earlier):
    return lax.optimization_barrier((value,) + earlier)[0]


def picked(row, width):
    col = jnp.transpose(jnp.broadcast_to(row, (128, BLOCK)))
    lane = lax.broadcasted_iota(jnp.int32, (BLOCK, 128), 1)
    parts = [
        jnp.where(col == lane + 128 * k, 1.0, 0.0).astype(jnp.bfloat16) for k in range(width // 128)
    ]
    return jnp.concatenate(parts, axis=1)


def pack_kernel(k_ref, v_ref, *refs, chunks):
    out_ref = refs[-1]
    line_rows = TILE * TCOLS
    pair = TILES * TILE
    for dest in range(16):
        group, head, kv = dest // 4, dest // 2 % 2, dest % 2
        from_ref = v_ref if kv else k_ref
        at = 0
        for c, line in itertools.product(range(chunks[0], chunks[1]), range(2)):
            cols = pl.ds((2 * (c - chunks[0]) + head) * HD, HD)
            rows = pl.ds(line * line_rows + group * pair, pair)
            out_ref[dest, pl.ds(at, pair), :] = from_ref[rows, cols]
            at += pair
        if len(refs) == 3:
            q_ref, places_ref = refs[:2]
            for h, line in itertools.product(range(4), range(2)):
                rows = pl.ds(line * line_rows + (dest // 2) * TILE, TILE)
                out_ref[dest, pl.ds(at, TILE), :] = q_ref[rows, pl.ds((4 * kv + h) * HD, HD)]
                at += TILE
            out_ref[dest, pl.ds(at, 16), :] = places_ref[...]


def pack(keys, values, chunks, *more):
    width = 2 * HD * (chunks[1] - chunks[0])
    part = pl.BlockSpec((BLOCK, width), lambda g: (0, 0))
    rows = 2 * TILES * TILE * (chunks[1] - chunks[0])
    more_specs = [pl.BlockSpec(m.shape, lambda g: (0, 0)) for m in more]
    if more:
        rows += 8 * TILE + 16
    if chunks[0]:
        keys, values = keys[:, chunks[0] * 2 * HD :], values[:, chunks[0] * 2 * HD :]
    return pl.pallas_call(
        functools.partial(pack_kernel, chunks=chunks),
        grid=(1,),
        in_specs=[part, part] + more_specs,
        out_specs=pl.BlockSpec((16, rows, HD), lambda g: (0, 0, 0)),
        out_shape=jax.ShapeDtypeStruct((16, rows, HD), jnp.bfloat16),
        compiler_params=pltpu.CompilerParams(vmem_limit_bytes=VMEM_LIMIT),
        cost_estimate=pl.CostEstimate(
            flops=0, bytes_accessed=2 * 16 * rows * HD * 2, transcendentals=0
        ),
        name="pack",
    )(keys, values, *more)


def order_kv_kernel(place_ref, rows_ref, out_ref):
    tile = rows_ref[...].reshape(TILE * TILE, HD)
    for b in range(2):
        hot = picked(place_ref[0, b : b + 1, :], TILE * TILE)
        rows = jnp.dot(hot, tile, preferred_element_type=jnp.float32).astype(jnp.bfloat16)
        out_ref[:, 0, b] = rows.reshape(4, PART, HD)


def order_kv(place, rows):
    chunks = rows.shape[1]
    return pl.pallas_call(
        order_kv_kernel,
        grid=(chunks, TILES),
        in_specs=[
            pl.BlockSpec((1, 2, BLOCK), lambda c, t: (t, 0, 0)),
            pl.BlockSpec((16, 1, 2, 1, TILE, HD), lambda c, t: (0, c, 0, t, 0, 0)),
        ],
        out_specs=pl.BlockSpec((4, 1, 2, PART, HD), lambda c, t: (0, c, t, 0, 0)),
        out_shape=jax.ShapeDtypeStruct((4, chunks, 2 * TILES, PART, HD), jnp.bfloat16),
        compiler_params=pltpu.CompilerParams(vmem_limit_bytes=VMEM_LIMIT),
        cost_estimate=pl.CostEstimate(
            flops=chunks * TILES * 4 * BLOCK * TILE * TILE * HD,
            bytes_accessed=chunks * TILES * 2**19,
            transcendentals=0,
        ),
        name="order_kv",
    )(place, rows)


def order_q_kernel(place_ref, rows_ref, out_ref):
    tile = rows_ref[...].reshape(TILE * TILE, HD)
    for b in range(2):
        hot = picked(place_ref[b : b + 1, :], TILE * TILE)
        out_ref[b, 0] = jnp.dot(hot, tile, preferred_element_type=jnp.float32).astype(jnp.bfloat16)


def order_q(place, rows):
    heads = rows.shape[1]
    return pl.pallas_call(
        order_q_kernel,
        grid=(heads,),
        in_specs=[
            pl.BlockSpec((2, BLOCK), lambda t: (0, 0)),
            pl.BlockSpec((16, 1, 2 * TILE, HD), lambda t: (0, t, 0, 0)),
        ],
        out_specs=pl.BlockSpec((2, 1, BLOCK, HD), lambda t: (0, t, 0, 0)),
        out_shape=jax.ShapeDtypeStruct((2, heads, BLOCK, HD), jnp.bfloat16),
        compiler_params=pltpu.CompilerParams(vmem_limit_bytes=VMEM_LIMIT),
        cost_estimate=pl.CostEstimate(
            flops=heads * 4 * BLOCK * TILE * TILE * HD, bytes_accessed=2**21, transcendentals=0
        ),
        name="order_q",
    )(place, rows)


def select_kernel(blocks_ref, held_ref, out_ref, sem):
    def send(step, carry):
        reader = step // SEL
        slot = step % SEL
        block = blocks_ref[reader, slot]
        col = lax.shift_right_logical(block, 5)
        line = lax.shift_right_logical(block, 2) & 7
        pltpu.make_async_copy(
            held_ref.at[line, col, block & 3], out_ref.at[reader, slot], sem
        ).start()
        return carry

    lax.fori_loop(0, 16 * SEL, send, 0)
    pltpu.make_async_copy(out_ref, out_ref, sem).wait()


def select(blocks, held):
    return pl.pallas_call(
        select_kernel,
        grid_spec=pltpu.PrefetchScalarGridSpec(
            num_scalar_prefetch=1,
            grid=(1,),
            in_specs=[pl.BlockSpec(memory_space=pl.ANY)],
            out_specs=pl.BlockSpec((16, SEL, PART, HD), lambda g, blocks: (0, 0, 0, 0)),
            scratch_shapes=[pltpu.SemaphoreType.DMA],
        ),
        out_shape=jax.ShapeDtypeStruct((16, SEL, PART, HD), jnp.bfloat16),
        compiler_params=pltpu.CompilerParams(vmem_limit_bytes=VMEM_LIMIT),
        cost_estimate=pl.CostEstimate(flops=0, bytes_accessed=2**23, transcendentals=0),
        name="select",
    )(blocks, held)


def attend_kernel(side_ref, q_ref, k_ref, v_ref, out_ref, *, scale):
    sub = BLOCK // 2
    for r in range(2):
        query = q_ref[0, 0, r * sub : (r + 1) * sub, :]
        top = jnp.full((sub, 1), -jnp.inf, jnp.float32)
        total = jnp.zeros((sub, 1), jnp.float32)
        mixed = jnp.zeros((sub, HD), jnp.float32)
        for c in range(4):
            keys = k_ref[c, 0, 0]
            values = v_ref[c, 0, 0]
            scores = lax.dot_general(
                query, keys, (((1,), (1,)), ((), ())), preferred_element_type=jnp.float32
            )
            peak = jnp.maximum(top, jnp.max(scores, axis=1, keepdims=True))
            weights = jnp.exp2(scores * scale - peak * scale)
            fade = jnp.exp2((top - peak) * scale)
            total = total * fade + jnp.sum(weights, axis=1, keepdims=True)
            mixed = mixed * fade + jnp.dot(
                weights.astype(jnp.bfloat16), values, preferred_element_type=jnp.float32
            )
            top = peak
        out_ref[r * sub : (r + 1) * sub, :] = (mixed / total).astype(jnp.bfloat16)


def attend(side, query, fetched, first):
    rows = SEL * PART
    spec = (4, 1, 1, rows, HD)
    heads = 2
    per_side = query.shape[1]
    return pl.pallas_call(
        functools.partial(attend_kernel, scale=math.log2(math.e) / math.sqrt(HD)),
        grid_spec=pltpu.PrefetchScalarGridSpec(
            num_scalar_prefetch=1,
            grid=(heads,),
            in_specs=[
                pl.BlockSpec(
                    (1, 1, BLOCK, HD),
                    lambda g, side: (first // per_side ^ side[0], first % per_side + g, 0, 0),
                ),
                pl.BlockSpec(spec, lambda g, side: (0, g, 0, 0, 0)),
                pl.BlockSpec(spec, lambda g, side: (0, g, 1, 0, 0)),
            ],
            out_specs=pl.BlockSpec((BLOCK, HD), lambda g, side: (0, g)),
        ),
        out_shape=jax.ShapeDtypeStruct((BLOCK, heads * HD), jnp.bfloat16),
        compiler_params=pltpu.CompilerParams(vmem_limit_bytes=VMEM_LIMIT),
        cost_estimate=pl.CostEstimate(
            flops=heads * 4 * BLOCK * 4 * rows * HD * 4,
            bytes_accessed=heads * 2**21,
            transcendentals=heads * BLOCK * 4 * rows,
        ),
        name="attend",
    )(side, query, fetched, fetched)


def body(q_raster, k_raster, v_raster, hilbert_order, key_blocks, out_weight):
    width = q_raster.shape[1]
    image_width = TILE * TCOLS
    core = lax.axis_index("core")
    swap = [(0, 1), (1, 0)]
    weight_far = lax.ppermute(out_weight, "core", swap)

    in_tile = hilbert_order // image_width % TILE * TILE + hilbert_order % image_width % TILE
    places = jnp.stack([in_tile // TILE, in_tile % TILE]).reshape(8, HD)
    listed = jnp.pad(key_blocks, ((0, 7), (0, HD - SEL)))
    places = jnp.concatenate([places, listed]).astype(jnp.bfloat16)
    by_chunk = (16, -1, 2, TILES, TILE, HD)
    kv_rows = 2 * TILES * TILE * LEAD
    lead = exchange(pack(k_raster, v_raster, (0, LEAD), q_raster, places), BAND)
    numbers = lead[:, -16:].astype(jnp.int32)
    band_places = numbers[:, :8].reshape(16, 2, BLOCK)
    band_places = (band_places[:, 0] * TILE + band_places[:, 1]).reshape(TCOLS, 2, BLOCK)
    line_pos = lax.axis_index("zl")
    place = lax.dynamic_slice_in_dim(band_places, line_pos * TILES, TILES, axis=0)
    ordered = order_kv(place, lead[:, :kv_rows].reshape(by_chunk))
    spread = exchange(ordered, "x")
    spreads = [spread[:, c] for c in range(LEAD)]

    lists = lax.dynamic_slice_in_dim(numbers[:, 8, :SEL], line_pos * 4, 4, axis=0)
    lists = [
        lax.ppermute(lists, "x", [(i, i ^ d) for i in range(4)]) if d else lists for d in range(4)
    ]
    lists = jnp.stack(lists)[lax.axis_index("x") ^ jnp.arange(4)].reshape(16, SEL)

    side = lax.axis_index("yl")
    tile_places = lax.dynamic_index_in_dim(band_places, lax.axis_index(("zl", "yh")), 0, False)
    tile_places = jnp.where(side == 0, tile_places, tile_places[::-1])
    q_ordered = order_q(tile_places, lead[:, kv_rows:-16].reshape(16, -1, 2 * TILE, HD))
    q_other = lax.ppermute(q_ordered[1], "yl", swap)
    query = jnp.stack([q_ordered[0], q_other])
    side = side.reshape(1)

    rest = exchange(after(pack(k_raster, v_raster, (LEAD, CHUNKS)), spread), BAND)
    ordered = order_kv(place, rest.reshape(by_chunk))
    later = exchange(after(ordered, lists, query), "x")
    spreads += [later[:, c] for c in range(CHUNKS - LEAD)]
    held = [lax.all_gather(part, LINE, axis=0) for part in spreads]

    half = BLOCK // 2
    results = [jnp.zeros((half, out_weight.shape[1]), jnp.float32)]
    for c in range(CHUNKS):
        ready = after(lists, *((results[c - 1],) if c > 1 else (later,)))
        got = exchange(select(ready, held[c]), PLANE)
        attended = attend(side, query, got.reshape(4, 2, 2, SEL * PART, HD), 2 * c)
        mine = lax.dynamic_slice_in_dim(attended, core * half, half, axis=0)
        theirs = lax.dynamic_slice_in_dim(attended, (1 - core) * half, half, axis=0)
        other = lax.ppermute(theirs, "core", swap)
        feats = slice(2 * c * HD, 2 * (c + 1) * HD)
        result = results[c] + jnp.dot(mine, out_weight[feats], preferred_element_type=jnp.float32)
        result += jnp.dot(other, weight_far[feats], preferred_element_type=jnp.float32)
        results.append(result)
    return results[-1].astype(jnp.bfloat16)


def solution(mesh):
    split = Mesh(mesh.devices.reshape(SIZES), SEQ + ("core",))
    placed = (
        P(SEQ, "core"),
        P(SEQ, "core"),
        P(SEQ, "core"),
        P(SEQ),
        P(SEQ, None),
        P("core", None),
    )
    return jax.shard_map(
        body, mesh=split, in_specs=placed, out_specs=P(SEQ + ("core",), None), check_vma=False
    )
```

time: 486 us -> 433 us (0.89)
  the two profiles are of different devices: /device:TPU:115 before, /device:TPU:1 now
where the time goes in v2:
time: 433 us; the launch traced here: 432 us
  waiting for transfers between devices  214 us (49%)
  starting transfers between devices  72.1 us (17%)
  Pallas kernels  66.9 us (15%)
  blocking collectives  25.8 us (6%)
  matrix products  18.7 us (4%)
  local copies, waits for them, and re-layouts  18.2 us (4%)
  between operations  13.6 us (3%)
    all_to_all x6, waiting for transfers between devices, exchange(): return lax.all_to_all(value, axes, split_axis=0, concat_axis=0, tiled=True)  109 us
    all_gather x4, waiting for transfers between devices, body(): held = [lax.all_gather(part, LINE, axis=0) for part in spreads]  86.2 us
    all_to_all x6, starting transfers between devices, exchange(): return lax.all_to_all(value, axes, split_axis=0, concat_axis=0, tiled=True)  47.4 us
    pallas_call x4, Pallas kernels, attend(): pl.pallas_call(functools.partial(attend_kernel, scale=math.log2(math.e) /...  39.6 us
    all_to_all x2, blocking collectives, exchange(): return lax.all_to_all(value, axes, split_axis=0, concat_axis=0, tiled=True)  25.8 us
    ppermute x4, starting transfers between devices, body(): other = lax.ppermute(theirs, 'core', swap)  15.4 us
    pallas_call x4, Pallas kernels, select(): pl.pallas_call(select_kernel, grid_spec=pltpu.PrefetchScalarGridSpec(num_...  14.8 us
    ppermute x1, waiting for transfers between devices, body(): q_other = lax.ppermute(q_ordered[1], 'yl', swap)  14.6 us
  transfers between devices with their start and end apart: 19, of which 12 were waited for; matrix products, arithmetic and copies ran while one was open for 5% of the time, Pallas kernels for 15%

profile of v2, /device:TPU:1, one launch (start us, length us, event | category | flops | bytes accessed | tf_op | source)
XLA Modules:
  0.0 431.5 jit_solution(10162017184569619880)
XLA Ops:
  13.2 9.2 %all-to-all-start = ((bf16[16,400,128]{2,1,0:T(8,128)(2,1)}), bf16[16,400,128]{2,1,0:T(8,128)(2,1)S(1)}, u32[]{:S(2)}, u32[]{:S(2)}) async-start(bf16[16,400,128]{2,1,0:T(8,128)(2,1)} %pack.2), calls=%async_computation | async-start | bytes 3276800 | tf_op jit(solution)/shard_map/all_to_all | solution.py:30
  22.4 33.4 %all-to-all-done = bf16[16,400,128]{2,1,0:T(8,128)(2,1)S(1)} async-done(((bf16[16,400,128]{2,1,0:T(8,128)(2,1)}), bf16[16,400,128]{2,1,0:T(8,128)(2,1)S(1)}, u32[]{:S(2)}, u32[]{:S(2)}) %all-to-all-start) | async-done | bytes 1638432 | tf_op jit(solution)/shard_map/all_to_all | solution.py:30
  59.9 10.9 %all_to_all.40 = bf16[4,1,4,128,128]{4,3,2,1,0:T(8,128)(2,1)} all-to-all(bf16[4,1,4,128,128]{4,3,2,1,0:T(8,128)(2,1)S(1)} %order_kv.2), channel_id=1, replica_groups=mesh['x'=4,'zh'=2,'zl'=4,'yh'=2,'yl'=2,'core'=2] {'x'}, dimensions={0} | all-to-all | bytes 1048576 | tf_op jit(solution)/shard_map/all_to_all | solution.py:30
  72.4 10.0 %all-to-all-start.2 = ((bf16[16,384,128]{2,1,0:T(8,128)(2,1)}), bf16[16,384,128]{2,1,0:T(8,128)(2,1)S(1)}, u32[]{:S(2)}, u32[]{:S(2)}) async-start(bf16[16,384,128]{2,1,0:T(8,128)(2,1)} %pack.3), calls=%async_computation.2 | async-start | bytes 3145728 | tf_op jit(solution)/shard_map/all_to_all | solution.py:30
  95.5 14.6 %collective-permute-done = bf16[4,512,128]{2,1,0:T(8,128)(2,1)S(1)} collective-permute-done((bf16[4,512,128]{2,1,0:T(8,128)(2,1)S(1)}, bf16[4,512,128]{2,1,0:T(8,128)(2,1)S(1)}, u32[]{:S(2)}, u32[]{:S(2)}) %collective-permute-start) | collective-permute-done | bytes 524320 | tf_op jit(solution)/shard_map/ppermute | solution.py:267
  112.0 16.9 %all-to-all-done.2 = bf16[16,384,128]{2,1,0:T(8,128)(2,1)S(1)} async-done(((bf16[16,384,128]{2,1,0:T(8,128)(2,1)}), bf16[16,384,128]{2,1,0:T(8,128)(2,1)S(1)}, u32[]{:S(2)}, u32[]{:S(2)}) %all-to-all-start.2) | async-done | bytes 1572896 | tf_op jit(solution)/shard_map/all_to_all | solution.py:30
  133.7 15.0 %all_to_all.41 = bf16[4,3,4,128,128]{4,3,2,1,0:T(8,128)(2,1)S(1)} all-to-all(bf16[4,3,4,128,128]{4,3,2,1,0:T(8,128)(2,1)S(1)} %order_kv.3), channel_id=1, replica_groups=mesh['x'=4,'zh'=2,'zl'=4,'yh'=2,'yl'=2,'core'=2] {'x'}, dimensions={0} | all-to-all | bytes 3145728 | tf_op jit(solution)/shard_map/all_to_all | solution.py:30
  150.7 6.3 %all-gather.9.cloned.1.call-done = bf16[32,1,4,128,128]{4,3,2,1,0:T(8,128)(2,1)} async-done(((bf16[4,1,4,128,128]{4,3,2,1,0:T(8,128)(2,1)}), bf16[32,1,4,128,128]{4,3,2,1,0:T(8,128)(2,1)}) %all-gather.9.cloned.1.call-update) | async-done | bytes 4194320 | tf_op jit(solution)/shard_map/all_gather | solution.py:275
  162.7 4.8 %all-to-all-start.4 = ((bf16[16,8,128,128]{3,2,1,0:T(8,128)(2,1)}), bf16[16,8,128,128]{3,2,1,0:T(8,128)(2,1)}, u32[]{:S(2)}, u32[]{:S(2)}) async-start(bf16[16,8,128,128]{3,2,1,0:T(8,128)(2,1)} %copy-done.3), calls=%async_computation.4 | async-start | bytes 8388608 | tf_op jit(solution)/shard_map/all_to_all | solution.py:30
  171.1 44.1 %all-gather.11.cloned.1.call-done = bf16[32,1,4,128,128]{4,3,2,1,0:T(8,128)(2,1)} async-done(((bf16[4,1,4,128,128]{4,3,2,1,0:T(8,128)(2,1)}), bf16[32,1,4,128,128]{4,3,2,1,0:T(8,128)(2,1)}) %all-gather.11.cloned.1.call-update) | async-done | bytes 4194320 | tf_op jit(solution)/shard_map/all_gather | solution.py:275
  220.8 6.6 %all-to-all-start.5 = ((bf16[16,8,128,128]{3,2,1,0:T(8,128)(2,1)}), bf16[16,8,128,128]{3,2,1,0:T(8,128)(2,1)}, u32[]{:S(2)}, u32[]{:S(2)}) async-start(bf16[16,8,128,128]{3,2,1,0:T(8,128)(2,1)} %copy-done), calls=%async_computation.5 | async-start | bytes 8388608 | tf_op jit(solution)/shard_map/all_to_all | solution.py:30
  228.0 9.8 %attend.4 = bf16[512,256]{1,0:T(8,128)(2,1)S(1)} custom-call(s32[1]{0:T(128)} %bitcast.side_ref, bf16[2,4,512,128]{3,2,1,0:T(8,128)(2,1)S(1)} %pad_maximum_fusion.q_ref, bf16[4,2,2,1024,128]{4,3,2,1,0:T(8,128)(2,1)} %bitcast.15.k_ref.v_ref, bf16[4,2,2,1024,128]{4,3,2,1,0:T(8,128)(2,1)} %bitcast.15.k_ref.v_ref), custom_call_target="tpu_custom_call" | custom-call | flops 8589934592 | bytes 4194304 | tf_op jit(solution)/shard_map/attend/pallas_call | solution.py:208
  243.6 26.8 %all-gather.13.cloned.1.call-done = bf16[32,1,4,128,128]{4,3,2,1,0:T(8,128)(2,1)} async-done(((bf16[4,1,4,128,128]{4,3,2,1,0:T(8,128)(2,1)}), bf16[32,1,4,128,128]{4,3,2,1,0:T(8,128)(2,1)}) %all-gather.13.cloned.1.call-update) | async-done | bytes 4194320 | tf_op jit(solution)/shard_map/all_gather | solution.py:275
  276.0 12.9 %all-to-all-done.5 = bf16[16,8,128,128]{3,2,1,0:T(8,128)(2,1)} async-done(((bf16[16,8,128,128]{3,2,1,0:T(8,128)(2,1)}), bf16[16,8,128,128]{3,2,1,0:T(8,128)(2,1)}, u32[]{:S(2)}, u32[]{:S(2)}) %all-to-all-start.5) | async-done | bytes 4194336 | tf_op jit(solution)/shard_map/all_to_all | solution.py:30
  288.9 9.7 %all-to-all-start.6 = ((bf16[16,8,128,128]{3,2,1,0:T(8,128)(2,1)}), bf16[16,8,128,128]{3,2,1,0:T(8,128)(2,1)}, u32[]{:S(2)}, u32[]{:S(2)}) async-start(bf16[16,8,128,128]{3,2,1,0:T(8,128)(2,1)} %copy-done.1), calls=%async_computation.6 | async-start | bytes 8388608 | tf_op jit(solution)/shard_map/all_to_all | solution.py:30
  298.7 10.0 %attend.5 = bf16[512,256]{1,0:T(8,128)(2,1)S(1)} custom-call(s32[1]{0:T(128)} %bitcast.side_ref, bf16[2,4,512,128]{3,2,1,0:T(8,128)(2,1)S(1)} %pad_maximum_fusion.q_ref, bf16[4,2,2,1024,128]{4,3,2,1,0:T(8,128)(2,1)} %bitcast.17.k_ref.v_ref, bf16[4,2,2,1024,128]{4,3,2,1,0:T(8,128)(2,1)} %bitcast.17.k_ref.v_ref), custom_call_target="tpu_custom_call" | custom-call | flops 8589934592 | bytes 4194304 | tf_op jit(solution)/shard_map/attend/pallas_call | solution.py:208
  316.4 9.1 %all-gather.15.cloned.1.call-done = bf16[32,1,4,128,128]{4,3,2,1,0:T(8,128)(2,1)} async-done(((bf16[4,1,4,128,128]{4,3,2,1,0:T(8,128)(2,1)}), bf16[32,1,4,128,128]{4,3,2,1,0:T(8,128)(2,1)}) %all-gather.15.cloned.1.call-update) | async-done | bytes 4194320 | tf_op jit(solution)/shard_map/all_gather | solution.py:275
  331.1 16.6 %all-to-all-done.6 = bf16[16,8,128,128]{3,2,1,0:T(8,128)(2,1)} async-done(((bf16[16,8,128,128]{3,2,1,0:T(8,128)(2,1)}), bf16[16,8,128,128]{3,2,1,0:T(8,128)(2,1)}, u32[]{:S(2)}, u32[]{:S(2)}) %all-to-all-start.6) | async-done | bytes 4194336 | tf_op jit(solution)/shard_map/all_to_all | solution.py:30
  347.7 7.0 %all-to-all-start.7 = ((bf16[16,8,128,128]{3,2,1,0:T(8,128)(2,1)}), bf16[16,8,128,128]{3,2,1,0:T(8,128)(2,1)}, u32[]{:S(2)}, u32[]{:S(2)}) async-start(bf16[16,8,128,128]{3,2,1,0:T(8,128)(2,1)} %copy-done.2), calls=%async_computation.7 | async-start | bytes 8388608 | tf_op jit(solution)/shard_map/all_to_all | solution.py:30
  354.8 10.0 %attend.6 = bf16[512,256]{1,0:T(8,128)(2,1)S(1)} custom-call(s32[1]{0:T(128)} %bitcast.side_ref, bf16[2,4,512,128]{3,2,1,0:T(8,128)(2,1)S(1)} %pad_maximum_fusion.q_ref, bf16[4,2,2,1024,128]{4,3,2,1,0:T(8,128)(2,1)} %bitcast.19.k_ref.v_ref, bf16[4,2,2,1024,128]{4,3,2,1,0:T(8,128)(2,1)} %bitcast.19.k_ref.v_ref), custom_call_target="tpu_custom_call" | custom-call | flops 8589934592 | bytes 4194304 | tf_op jit(solution)/shard_map/attend/pallas_call | solution.py:208
  364.8 5.1 %collective-permute-start.7 = (bf16[256,256]{1,0:T(8,128)(2,1)S(1)}, bf16[256,256]{1,0:T(8,128)(2,1)S(1)}, u32[]{:S(2)}, u32[]{:S(2)}) collective-permute-start(bf16[256,256]{1,0:T(8,128)(2,1)S(1)} %constant_dynamic-slice_fusion.1), channel_id=1, source_target_pairs={{0,1},{1,0},{2,3},{3,2},{4,5},{5,4},{6,7},{7,6},{8,9},{9,8},{10,11... | collective-permute-start | bytes 393224 | tf_op jit(solution)/shard_map/ppermute | solution.py:285
  372.9 29.6 %all-to-all-done.7 = bf16[16,8,128,128]{3,2,1,0:T(8,128)(2,1)} async-done(((bf16[16,8,128,128]{3,2,1,0:T(8,128)(2,1)}), bf16[16,8,128,128]{3,2,1,0:T(8,128)(2,1)}, u32[]{:S(2)}, u32[]{:S(2)}) %all-to-all-start.7) | async-done | bytes 4194336 | tf_op jit(solution)/shard_map/all_to_all | solution.py:30
  402.5 9.8 %attend.7 = bf16[512,256]{1,0:T(8,128)(2,1)S(1)} custom-call(s32[1]{0:T(128)} %bitcast.side_ref, bf16[2,4,512,128]{3,2,1,0:T(8,128)(2,1)S(1)} %pad_maximum_fusion.q_ref, bf16[4,2,2,1024,128]{4,3,2,1,0:T(8,128)(2,1)} %bitcast.21.k_ref.v_ref, bf16[4,2,2,1024,128]{4,3,2,1,0:T(8,128)(2,1)} %bitcast.21.k_ref.v_ref), custom_call_target="tpu_custom_call" | custom-call | flops 8589934592 | bytes 4194304 | tf_op jit(solution)/shard_map/attend/pallas_call | solution.py:208
  414.2 6.4 %collective-permute-start.8 = (bf16[256,256]{1,0:T(8,128)(2,1)S(1)}, bf16[256,256]{1,0:T(8,128)(2,1)S(1)}, u32[]{:S(2)}, u32[]{:S(2)}) collective-permute-start(bf16[256,256]{1,0:T(8,128)(2,1)S(1)} %constant_dynamic-slice_fusion), channel_id=1, source_target_pairs={{0,1},{1,0},{2,3},{3,2},{4,5},{5,4},{6,7},{7,6},{8,9},{9,8},{10,11... | collective-permute-start | bytes 393224 | tf_op jit(solution)/shard_map/ppermute | solution.py:285
  (104 shorter events, 83.3 us)
Async XLA Ops:
  13.2 42.7 %all-to-all-start = ((bf16[16,400,128]{2,1,0:T(8,128)(2,1)}), bf16[16,400,128]{2,1,0:T(8,128)(2,1)S(1)}, u32[]{:S(2)}, u32[]{:S(2)}) async-start(bf16[16,400,128]{2,1,0:T(8,128)(2,1)} %pack.2), calls=%async_computation | async-start | bytes 3276800 | tf_op jit(solution)/shard_map/all_to_all | solution.py:30
  22.4 134.7 %all-gather.9.cloned.1.call-start = ((), (), s32[]{:S(2)}) async-start(), calls=%async_computation.8 | async-start | bytes 4718592 | tf_op jit(solution)/shard_map/all_gather | solution.py:275
  57.0 13.7 %copy-start.5 = (bf16[512,1024]{1,0:T(8,128)(2,1)S(1)}, bf16[512,1024]{1,0:T(8,128)(2,1)}, u32[]{:S(2)}) copy-start(bf16[512,1024]{1,0:T(8,128)(2,1)} %k_ref.1) | copy-start | bytes 3145732
  58.2 12.6 %copy-start.7 = (bf16[512,1024]{1,0:T(8,128)(2,1)S(1)}, bf16[512,1024]{1,0:T(8,128)(2,1)}, u32[]{:S(2)}) copy-start(bf16[512,1024]{1,0:T(8,128)(2,1)} %v_ref.1) | copy-start | bytes 3145732
  72.4 56.6 %all-to-all-start.2 = ((bf16[16,384,128]{2,1,0:T(8,128)(2,1)}), bf16[16,384,128]{2,1,0:T(8,128)(2,1)S(1)}, u32[]{:S(2)}, u32[]{:S(2)}) async-start(bf16[16,384,128]{2,1,0:T(8,128)(2,1)} %pack.3), calls=%async_computation.2 | async-start | bytes 3145728 | tf_op jit(solution)/shard_map/all_to_all | solution.py:30
  82.3 132.8 %all-gather.11.cloned.1.call-start = ((), (), s32[]{:S(2)}) async-start(), calls=%async_computation.9 | async-start | bytes 4718592 | tf_op jit(solution)/shard_map/all_gather | solution.py:275
  87.2 22.9 %collective-permute-start = (bf16[4,512,128]{2,1,0:T(8,128)(2,1)S(1)}, bf16[4,512,128]{2,1,0:T(8,128)(2,1)S(1)}, u32[]{:S(2)}, u32[]{:S(2)}) collective-permute-start(bf16[4,512,128]{2,1,0:T(8,128)(2,1)S(1)} %get-tuple-element.21), channel_id=1, source_target_pairs={{0,2},{2,0},{1,3},{3,1},{4,6},{6,4},{5,7},{7,5},{8,10},{10,8},{9,1... | collective-permute-start | bytes 1572872 | tf_op jit(solution)/shard_map/ppermute | solution.py:267
  88.7 3.9 collective-permute-start.1
  89.1 4.2 collective-permute-start.2
  90.8 4.0 collective-permute-start.3
  149.9 120.4 %all-gather.13.cloned.1.call-start = ((), (), s32[]{:S(2)}) async-start(), calls=%async_computation.10 | async-start | bytes 4718592 | tf_op jit(solution)/shard_map/all_gather | solution.py:275
  162.7 58.2 %all-to-all-start.4 = ((bf16[16,8,128,128]{3,2,1,0:T(8,128)(2,1)}), bf16[16,8,128,128]{3,2,1,0:T(8,128)(2,1)}, u32[]{:S(2)}, u32[]{:S(2)}) async-start(bf16[16,8,128,128]{3,2,1,0:T(8,128)(2,1)} %copy-done.3), calls=%async_computation.4 | async-start | bytes 8388608 | tf_op jit(solution)/shard_map/all_to_all | solution.py:30
  167.5 73.1 %collective-permute-start.5 = (bf16[1024,2048]{1,0:T(8,128)(2,1)}, bf16[1024,2048]{1,0:T(8,128)(2,1)}, u32[]{:S(2)}, u32[]{:S(2)}) collective-permute-start(bf16[1024,2048]{1,0:T(8,128)(2,1)} %param.11), channel_id=1, source_target_pairs={{0,1},{1,0},{2,3},{3,2},{4,5},{5,4},{6,7},{7,6},{8,9},{9,8},{10,11... | collective-permute-start | bytes 12582920 | tf_op jit(solution)/shard_map/ppermute | solution.py:239
  220.8 68.1 %all-to-all-start.5 = ((bf16[16,8,128,128]{3,2,1,0:T(8,128)(2,1)}), bf16[16,8,128,128]{3,2,1,0:T(8,128)(2,1)}, u32[]{:S(2)}, u32[]{:S(2)}) async-start(bf16[16,8,128,128]{3,2,1,0:T(8,128)(2,1)} %copy-done), calls=%async_computation.5 | async-start | bytes 8388608 | tf_op jit(solution)/shard_map/all_to_all | solution.py:30
  227.4 98.0 %all-gather.15.cloned.1.call-start = ((), (), s32[]{:S(2)}) async-start(), calls=%async_computation.11 | async-start | bytes 4718592 | tf_op jit(solution)/shard_map/all_gather | solution.py:275
  237.9 2.7 collective-permute-start.4
  288.9 58.8 %all-to-all-start.6 = ((bf16[16,8,128,128]{3,2,1,0:T(8,128)(2,1)}), bf16[16,8,128,128]{3,2,1,0:T(8,128)(2,1)}, u32[]{:S(2)}, u32[]{:S(2)}) async-start(bf16[16,8,128,128]{3,2,1,0:T(8,128)(2,1)} %copy-done.1), calls=%async_computation.6 | async-start | bytes 8388608 | tf_op jit(solution)/shard_map/all_to_all | solution.py:30
  298.7 13.0 %copy-start.11 = (f32[256,2048]{1,0:T(8,128)S(1)}, f32[256,2048]{1,0:T(8,128)}, u32[]{:S(2)}) copy-start(f32[256,2048]{1,0:T(8,128)} %convolution_add_fusion.5) | copy-start | bytes 6291460
  308.7 4.6 %collective-permute-start.6 = (bf16[256,256]{1,0:T(8,128)(2,1)S(1)}, bf16[256,256]{1,0:T(8,128)(2,1)S(1)}, u32[]{:S(2)}, u32[]{:S(2)}) collective-permute-start(bf16[256,256]{1,0:T(8,128)(2,1)S(1)} %constant_dynamic-slice_fusion.2), channel_id=1, source_target_pairs={{0,1},{1,0},{2,3},{3,2},{4,5},{5,4},{6,7},{7,6},{8,9},{9,8},{10,11... | collective-permute-start | bytes 393224 | tf_op jit(solution)/shard_map/ppermute | solution.py:285
  347.7 54.8 %all-to-all-start.7 = ((bf16[16,8,128,128]{3,2,1,0:T(8,128)(2,1)}), bf16[16,8,128,128]{3,2,1,0:T(8,128)(2,1)}, u32[]{:S(2)}, u32[]{:S(2)}) async-start(bf16[16,8,128,128]{3,2,1,0:T(8,128)(2,1)} %copy-done.2), calls=%async_computation.7 | async-start | bytes 8388608 | tf_op jit(solution)/shard_map/all_to_all | solution.py:30
  354.8 15.1 %copy-start.10 = (f32[256,2048]{1,0:T(8,128)S(1)}, f32[256,2048]{1,0:T(8,128)}, u32[]{:S(2)}) copy-start(f32[256,2048]{1,0:T(8,128)} %convolution_add_fusion.3) | copy-start | bytes 6291460
  364.8 55.8 %collective-permute-start.7 = (bf16[256,256]{1,0:T(8,128)(2,1)S(1)}, bf16[256,256]{1,0:T(8,128)(2,1)S(1)}, u32[]{:S(2)}, u32[]{:S(2)}) collective-permute-start(bf16[256,256]{1,0:T(8,128)(2,1)S(1)} %constant_dynamic-slice_fusion.1), channel_id=1, source_target_pairs={{0,1},{1,0},{2,3},{3,2},{4,5},{5,4},{6,7},{7,6},{8,9},{9,8},{10,11... | collective-permute-start | bytes 393224 | tf_op jit(solution)/shard_map/ppermute | solution.py:285
  412.3 8.3 %copy-start.9 = (f32[256,2048]{1,0:T(8,128)S(1)}, f32[256,2048]{1,0:T(8,128)}, u32[]{:S(2)}) copy-start(f32[256,2048]{1,0:T(8,128)} %convolution_add_fusion.2) | copy-start | bytes 6291460
  414.2 8.1 %collective-permute-start.8 = (bf16[256,256]{1,0:T(8,128)(2,1)S(1)}, bf16[256,256]{1,0:T(8,128)(2,1)S(1)}, u32[]{:S(2)}, u32[]{:S(2)}) collective-permute-start(bf16[256,256]{1,0:T(8,128)(2,1)S(1)} %constant_dynamic-slice_fusion), channel_id=1, source_target_pairs={{0,1},{1,0},{2,3},{3,2},{4,5},{5,4},{6,7},{7,6},{8,9},{9,8},{10,11... | collective-permute-start | bytes 393224 | tf_op jit(solution)/shard_map/ppermute | solution.py:285
  (9 other events, 13.5 us)
Sparse Core Ops, SparseCore 0:
  70.9 86.0 all-gather.8
  158.8 56.2 all-gather.10
  216.9 53.4 all-gather.12
  272.0 53.4 all-gather.14

commit v3 on v2

--- a/solution.py
+++ b/solution.py
@@ -32,6 +32,14 @@
 
 def after(value, *earlier):
     return lax.optimization_barrier((value,) + earlier)[0]
+
+
+def swapped(pieces, axes):
+    moved = [
+        lax.ppermute(pieces[d], axes, [(i, i ^ d) for i in range(4)]) if d else pieces[0]
+        for d in range(4)
+    ]
+    return jnp.stack(moved)
 
 
 def picked(row, width):
@@ -143,68 +151,68 @@
     )(place, rows)
 
 
-def select_kernel(blocks_ref, held_ref, out_ref, sem):
-    def send(step, carry):
-        reader = step // SEL
-        slot = step % SEL
-        block = blocks_ref[reader, slot]
-        col = lax.shift_right_logical(block, 5)
-        line = lax.shift_right_logical(block, 2) & 7
-        pltpu.make_async_copy(
-            held_ref.at[line, col, block & 3], out_ref.at[reader, slot], sem
-        ).start()
+def select_kernel(blocks_ref, flip_ref, held_ref, out_ref, sem):
+    def send(reader, carry):
+        for slot in range(1, SEL):
+            block = blocks_ref[reader, slot]
+            col = lax.shift_right_logical(block, 5) ^ flip_ref[0]
+            line = lax.shift_right_logical(block, 2) & 7
+            pltpu.make_async_copy(
+                held_ref.at[line, col, block & 3], out_ref.at[reader, slot - 1], sem
+            ).start()
         return carry
 
-    lax.fori_loop(0, 16 * SEL, send, 0)
+    lax.fori_loop(0, 16, send, 0)
     pltpu.make_async_copy(out_ref, out_ref, sem).wait()
 
 
-def select(blocks, held):
+def select(blocks, flip, held):
+    shape = (16, SEL - 1, PART, HD)
     return pl.pallas_call(
         select_kernel,
         grid_spec=pltpu.PrefetchScalarGridSpec(
-            num_scalar_prefetch=1,
+            num_scalar_prefetch=2,
             grid=(1,),
             in_specs=[pl.BlockSpec(memory_space=pl.ANY)],
-            out_specs=pl.BlockSpec((16, SEL, PART, HD), lambda g, blocks: (0, 0, 0, 0)),
+            out_specs=pl.BlockSpec(shape, lambda g, blocks, flip: (0, 0, 0, 0)),
             scratch_shapes=[pltpu.SemaphoreType.DMA],
         ),
-        out_shape=jax.ShapeDtypeStruct((16, SEL, PART, HD), jnp.bfloat16),
+        out_shape=jax.ShapeDtypeStruct(shape, jnp.bfloat16),
         compiler_params=pltpu.CompilerParams(vmem_limit_bytes=VMEM_LIMIT),
         cost_estimate=pl.CostEstimate(flops=0, bytes_accessed=2**23, transcendentals=0),
         name="select",
-    )(blocks, held)
-
-
-def attend_kernel(side_ref, q_ref, k_ref, v_ref, out_ref, *, scale):
-    sub = BLOCK // 2
-    for r in range(2):
-        query = q_ref[0, 0, r * sub : (r + 1) * sub, :]
-        top = jnp.full((sub, 1), -jnp.inf, jnp.float32)
-        total = jnp.zeros((sub, 1), jnp.float32)
-        mixed = jnp.zeros((sub, HD), jnp.float32)
-        for c in range(4):
-            keys = k_ref[c, 0, 0]
-            values = v_ref[c, 0, 0]
-            scores = lax.dot_general(
-                query, keys, (((1,), (1,)), ((), ())), preferred_element_type=jnp.float32
-            )
-            peak = jnp.maximum(top, jnp.max(scores, axis=1, keepdims=True))
-            weights = jnp.exp2(scores * scale - peak * scale)
-            fade = jnp.exp2((top - peak) * scale)
-            total = total * fade + jnp.sum(weights, axis=1, keepdims=True)
-            mixed = mixed * fade + jnp.dot(
-                weights.astype(jnp.bfloat16), values, preferred_element_type=jnp.float32
-            )
-            top = peak
-        out_ref[r * sub : (r + 1) * sub, :] = (mixed / total).astype(jnp.bfloat16)
-
-
-def attend(side, query, fetched, first):
-    rows = SEL * PART
+    )(blocks, flip, held)
+
+
+def attend_kernel(pos_ref, q_ref, k_ref, v_ref, own_k_ref, own_v_ref, out_ref, *, scale):
+    query = q_ref[0, 0]
+    top = jnp.full((BLOCK, 1), -jnp.inf, jnp.float32)
+    total = jnp.zeros((BLOCK, 1), jnp.float32)
+    mixed = jnp.zeros((BLOCK, HD), jnp.float32)
+    for c in range(4):
+        keys = jnp.concatenate([k_ref[c, 0, 0], own_k_ref[0, c, 0]])
+        values = jnp.concatenate([v_ref[c, 0, 0], own_v_ref[0, c, 0]])
+        scores = lax.dot_general(
+            query, keys, (((1,), (1,)), ((), ())), preferred_element_type=jnp.float32
+        )
+        peak = jnp.maximum(top, jnp.max(scores, axis=1, keepdims=True))
+        weights = jnp.exp2(scores * scale - peak * scale)
+        fade = jnp.exp2((top - peak) * scale)
+        total = total * fade + jnp.sum(weights, axis=1, keepdims=True)
+        mixed = mixed * fade + jnp.dot(
+            weights.astype(jnp.bfloat16), values, preferred_element_type=jnp.float32
+        )
+        top = peak
+    out_ref[...] = (mixed / total).astype(jnp.bfloat16)
+
+
+def attend(pos, query, fetched, own, chunk):
+    rows = (SEL - 1) * PART
     spec = (4, 1, 1, rows, HD)
+    own_spec = (1, 4, 1, PART, HD)
     heads = 2
     per_side = query.shape[1]
+    first = heads * chunk
     return pl.pallas_call(
         functools.partial(attend_kernel, scale=math.log2(math.e) / math.sqrt(HD)),
         grid_spec=pltpu.PrefetchScalarGridSpec(
@@ -213,22 +221,24 @@
             in_specs=[
                 pl.BlockSpec(
                     (1, 1, BLOCK, HD),
-                    lambda g, side: (first // per_side ^ side[0], first % per_side + g, 0, 0),
+                    lambda g, pos: (first // per_side ^ (pos[0] & 1), first % per_side + g, 0, 0),
                 ),
-                pl.BlockSpec(spec, lambda g, side: (0, g, 0, 0, 0)),
-                pl.BlockSpec(spec, lambda g, side: (0, g, 1, 0, 0)),
+                pl.BlockSpec(spec, lambda g, pos: (0, g, 0, 0, 0)),
+                pl.BlockSpec(spec, lambda g, pos: (0, g, 1, 0, 0)),
+                pl.BlockSpec(own_spec, lambda g, pos: ((2 * g) ^ pos[0], 0, chunk, 0, 0)),
+                pl.BlockSpec(own_spec, lambda g, pos: ((2 * g + 1) ^ pos[0], 0, chunk, 0, 0)),
             ],
-            out_specs=pl.BlockSpec((BLOCK, HD), lambda g, side: (0, g)),
+            out_specs=pl.BlockSpec((BLOCK, HD), lambda g, pos: (0, g)),
         ),
         out_shape=jax.ShapeDtypeStruct((BLOCK, heads * HD), jnp.bfloat16),
         compiler_params=pltpu.CompilerParams(vmem_limit_bytes=VMEM_LIMIT),
         cost_estimate=pl.CostEstimate(
-            flops=heads * 4 * BLOCK * 4 * rows * HD * 4,
+            flops=heads * 4 * BLOCK * BLOCK * SEL * HD * 4,
             bytes_accessed=heads * 2**21,
-            transcendentals=heads * BLOCK * 4 * rows,
+            transcendentals=heads * BLOCK * BLOCK * SEL,
         ),
         name="attend",
-    )(side, query, fetched, fetched)
+    )(pos, query, fetched, fetched, own, own)
 
 
 def body(q_raster, k_raster, v_raster, hilbert_order, key_blocks, out_weight):
@@ -250,15 +260,13 @@
     band_places = (band_places[:, 0] * TILE + band_places[:, 1]).reshape(TCOLS, 2, BLOCK)
     line_pos = lax.axis_index("zl")
     place = lax.dynamic_slice_in_dim(band_places, line_pos * TILES, TILES, axis=0)
-    ordered = order_kv(place, lead[:, :kv_rows].reshape(by_chunk))
-    spread = exchange(ordered, "x")
+    lead_ordered = order_kv(place, lead[:, :kv_rows].reshape(by_chunk))
+    spread = swapped(lead_ordered, "x")
     spreads = [spread[:, c] for c in range(LEAD)]
 
     lists = lax.dynamic_slice_in_dim(numbers[:, 8, :SEL], line_pos * 4, 4, axis=0)
-    lists = [
-        lax.ppermute(lists, "x", [(i, i ^ d) for i in range(4)]) if d else lists for d in range(4)
-    ]
-    lists = jnp.stack(lists)[lax.axis_index("x") ^ jnp.arange(4)].reshape(16, SEL)
+    lists = swapped(jnp.broadcast_to(lists[None], (4, 4, SEL)), "x")
+    lists = lists[lax.axis_index("x") ^ jnp.arange(4)].reshape(16, SEL)
 
     side = lax.axis_index("yl")
     tile_places = lax.dynamic_index_in_dim(band_places, lax.axis_index(("zl", "yh")), 0, False)
@@ -266,11 +274,17 @@
     q_ordered = order_q(tile_places, lead[:, kv_rows:-16].reshape(16, -1, 2 * TILE, HD))
     q_other = lax.ppermute(q_ordered[1], "yl", swap)
     query = jnp.stack([q_ordered[0], q_other])
-    side = side.reshape(1)
+    flip = lax.axis_index("x").reshape(1)
 
     rest = exchange(after(pack(k_raster, v_raster, (LEAD, CHUNKS)), spread), BAND)
     ordered = order_kv(place, rest.reshape(by_chunk))
-    later = exchange(after(ordered, lists, query), "x")
+    pos = lax.axis_index(("yh", "yl"))
+    ordered, _, _ = lax.optimization_barrier((ordered, lists, query))
+    every = jnp.concatenate([lead_ordered, ordered], axis=1)
+    own = [lax.dynamic_index_in_dim(every, pos ^ d, 2, False) for d in range(4)]
+    later, own = lax.optimization_barrier(
+        (swapped(ordered, "x"), swapped(own, ("yh", "yl")))
+    )
     spreads += [later[:, c] for c in range(CHUNKS - LEAD)]
     held = [lax.all_gather(part, LINE, axis=0) for part in spreads]
 
@@ -278,8 +292,9 @@
     results = [jnp.zeros((half, out_weight.shape[1]), jnp.float32)]
     for c in range(CHUNKS):
         ready = after(lists, *((results[c - 1],) if c > 1 else (later,)))
-        got = exchange(select(ready, held[c]), PLANE)
-        attended = attend(side, query, got.reshape(4, 2, 2, SEL * PART, HD), 2 * c)
+        got = exchange(select(ready, flip, held[c]), PLANE)
+        got = got.reshape(4, 2, 2, (SEL - 1) * PART, HD)
+        attended = attend(pos.reshape(1), query, got, own, c)
         mine = lax.dynamic_slice_in_dim(attended, core * half, half, axis=0)
         theirs = lax.dynamic_slice_in_dim(attended, (1 - core) * half, half, axis=0)
         other = lax.ppermute(theirs, "core", swap)

time: 433 us -> 421 us (0.972)
  blocking collectives: 25.8 us -> 0 us
  starting transfers between devices: 72.1 us -> 87.5 us
  Pallas kernels: 66.9 us -> 57.8 us
    all_to_all x2 -> x0, blocking collectives: 25.8 us -> none  [exchange(): return lax.all_to_all(value, axes, split_axis=0, concat_axis=0, tiled=True)]
    all_to_all x6, waiting for transfers between devices: 109 us -> 86 us  [exchange(): return lax.all_to_all(value, axes, split_axis=0, concat_axis=0, tiled=True)]
    ppermute x3 -> x12, waiting for transfers between devices: 2.26 us -> 22.3 us  [swapped(): lax.ppermute(pieces[d], axes, [(i, i ^ d) for i in range(4)])]
    ppermute x3 -> x12, starting transfers between devices: 3.95 us -> 12.9 us  [swapped(): lax.ppermute(pieces[d], axes, [(i, i ^ d) for i in range(4)])]
    all_gather x4, waiting for transfers between devices: 86.2 us -> 94.3 us  [body(): held = [lax.all_gather(part, LINE, axis=0) for part in spreads]]
    pallas_call x4, Pallas kernels: 39.6 us -> 33.3 us  [attend(): pl.pallas_call(functools.partial(attend_kernel, scale=math.log2(math.e) /...]
    all_to_all x6, starting transfers between devices: 47.4 us -> 53.1 us  [exchange(): return lax.all_to_all(value, axes, split_axis=0, concat_axis=0, tiled=True)]
    unnamed x28 -> x32, local copies, waits for them, and re-layouts: 13.3 us -> 14.5 us
  transfers between devices with their start and end apart: 19 -> 28, of which waited for: 12 -> 17; matrix products, arithmetic and copies ran while one was open for 5% -> 6% of each run, Pallas kernels for 15% -> 13%
where the time goes in v3:
time: 421 us; the launch traced here: 418 us
  waiting for transfers between devices  215 us (51%)
  starting transfers between devices  87.5 us (21%)
  Pallas kernels  57.8 us (14%)
  local copies, waits for them, and re-layouts  20.1 us (5%)
  matrix products  18.6 us (4%)
  between operations  13.7 us (3%)
  other arithmetic  5.12 us (1%)
    all_gather x4, waiting for transfers between devices, body(): held = [lax.all_gather(part, LINE, axis=0) for part in spreads]  94.3 us
    all_to_all x6, waiting for transfers between devices, exchange(): return lax.all_to_all(value, axes, split_axis=0, concat_axis=0, tiled=True)  86 us
    all_to_all x6, starting transfers between devices, exchange(): return lax.all_to_all(value, axes, split_axis=0, concat_axis=0, tiled=True)  53.1 us
    pallas_call x4, Pallas kernels, attend(): pl.pallas_call(functools.partial(attend_kernel, scale=math.log2(math.e) /...  33.3 us
    ppermute x12, waiting for transfers between devices, swapped(): lax.ppermute(pieces[d], axes, [(i, i ^ d) for i in range(4)])  22.3 us
    unnamed x32, local copies, waits for them, and re-layouts  14.5 us
    ppermute x4, starting transfers between devices, body(): other = lax.ppermute(theirs, 'core', swap)  13 us
    ppermute x12, starting transfers between devices, swapped(): lax.ppermute(pieces[d], axes, [(i, i ^ d) for i in range(4)])  12.9 us
  transfers between devices with their start and end apart: 28, of which 17 were waited for; matrix products, arithmetic and copies ran while one was open for 6% of the time, Pallas kernels for 13%

profile of v3, /device:TPU:1, one launch (start us, length us, event | category | flops | bytes accessed | tf_op | source)
XLA Modules:
  0.0 418.0 jit_solution(15040401072019382276)
XLA Ops:
  13.2 9.2 %all-to-all-start = ((bf16[16,400,128]{2,1,0:T(8,128)(2,1)}), bf16[16,400,128]{2,1,0:T(8,128)(2,1)S(1)}, u32[]{:S(2)}, u32[]{:S(2)}) async-start(bf16[16,400,128]{2,1,0:T(8,128)(2,1)} %pack.2), calls=%async_computation | async-start | bytes 3276800 | tf_op jit(solution)/shard_map/all_to_all | solution.py:30
  22.4 33.4 %all-to-all-done = bf16[16,400,128]{2,1,0:T(8,128)(2,1)S(1)} async-done(((bf16[16,400,128]{2,1,0:T(8,128)(2,1)}), bf16[16,400,128]{2,1,0:T(8,128)(2,1)S(1)}, u32[]{:S(2)}, u32[]{:S(2)}) %all-to-all-start) | async-done | bytes 1638432 | tf_op jit(solution)/shard_map/all_to_all | solution.py:30
  62.7 3.6 collective-permute-done.5
  70.2 11.4 %all-to-all-start.1 = ((bf16[16,384,128]{2,1,0:T(8,128)(2,1)}), bf16[16,384,128]{2,1,0:T(8,128)(2,1)S(1)}, u32[]{:S(2)}, u32[]{:S(2)}) async-start(bf16[16,384,128]{2,1,0:T(8,128)(2,1)} %pack.3), calls=%async_computation.1 | async-start | bytes 3145728 | tf_op jit(solution)/shard_map/all_to_all | solution.py:30
  95.5 11.8 %collective-permute-done = bf16[4,512,128]{2,1,0:T(8,128)(2,1)} collective-permute-done((bf16[4,512,128]{2,1,0:T(8,128)(2,1)}, bf16[4,512,128]{2,1,0:T(8,128)(2,1)}, u32[]{:S(2)}, u32[]{:S(2)}) %collective-permute-start) | collective-permute-done | bytes 524320 | tf_op jit(solution)/shard_map/ppermute | solution.py:275
  109.4 22.0 %all-to-all-done.1 = bf16[16,384,128]{2,1,0:T(8,128)(2,1)S(1)} async-done(((bf16[16,384,128]{2,1,0:T(8,128)(2,1)}), bf16[16,384,128]{2,1,0:T(8,128)(2,1)S(1)}, u32[]{:S(2)}, u32[]{:S(2)}) %all-to-all-start.1) | async-done | bytes 1572896 | tf_op jit(solution)/shard_map/all_to_all | solution.py:30
  134.0 4.8 %order_kv.3 = bf16[4,3,4,128,128]{4,3,2,1,0:T(8,128)(2,1)S(1)} custom-call(s32[2,2,512]{2,1,0:T(2,128)S(1)} %constant_dynamic-slice_fusion.4.place_ref, bf16[16,3,2,2,32,128]{5,4,3,2,1,0:T(8,128)(2,1)S(1)} %bitcast.63), custom_call_target="tpu_custom_call" | custom-call | flops 1610612736 | bytes 3145728 | tf_op jit(solution)/shard_map/order_kv/pallas_call | solution.py:109
  147.8 5.1 %collective-permute-done.8 = bf16[3,4,128,128]{3,2,1,0:T(8,128)(2,1)S(1)} collective-permute-done((bf16[3,4,128,128]{3,2,1,0:T(8,128)(2,1)}, bf16[3,4,128,128]{3,2,1,0:T(8,128)(2,1)S(1)}, u32[]{:S(2)}, u32[]{:S(2)}) %collective-permute-start.8) | collective-permute-done | bytes 393248 | tf_op jit(solution)/shard_map/ppermute | solution.py:39
  155.0 5.2 %collective-permute-done.11 = bf16[4,4,128,128]{3,2,1,0:T(8,128)(2,1)S(1)} collective-permute-done((bf16[4,4,128,128]{3,2,1,0:T(8,128)(2,1)S(1)}, bf16[4,4,128,128]{3,2,1,0:T(8,128)(2,1)S(1)}, u32[]{:S(2)}, u32[]{:S(2)}) %collective-permute-start.11) | collective-permute-done | bytes 524320 | tf_op jit(solution)/shard_map/ppermute | solution.py:39
  167.3 9.2 %all-to-all-start.2 = ((bf16[16,7,128,128]{3,2,1,0:T(8,128)(2,1)}), bf16[16,7,128,128]{3,2,1,0:T(8,128)(2,1)}, u32[]{:S(2)}, u32[]{:S(2)}) async-start(bf16[16,7,128,128]{3,2,1,0:T(8,128)(2,1)} %copy-done.2), calls=%async_computation.2 | async-start | bytes 7340032 | tf_op jit(solution)/shard_map/all_to_all | solution.py:30
  176.6 7.0 %collective-permute-start.14 = (bf16[1024,2048]{1,0:T(8,128)(2,1)}, bf16[1024,2048]{1,0:T(8,128)(2,1)}, u32[]{:S(2)}, u32[]{:S(2)}) collective-permute-start(bf16[1024,2048]{1,0:T(8,128)(2,1)} %param.11), channel_id=1, source_target_pairs={{0,1},{1,0},{2,3},{3,2},{4,5},{5,4},{6,7},{7,6},{8,9},{9,8},{10,11... | collective-permute-start | bytes 12582920 | tf_op jit(solution)/shard_map/ppermute | solution.py:249
  183.6 43.0 %all-gather.11.cloned.1.call-done = bf16[32,1,4,128,128]{4,3,2,1,0:T(8,128)(2,1)} async-done(((bf16[4,1,4,128,128]{4,3,2,1,0:T(8,128)(2,1)}), bf16[32,1,4,128,128]{4,3,2,1,0:T(8,128)(2,1)}) %all-gather.11.cloned.1.call-update) | async-done | bytes 4194320 | tf_op jit(solution)/shard_map/all_gather | solution.py:289
  231.4 7.0 %all-to-all-start.3 = ((bf16[16,7,128,128]{3,2,1,0:T(8,128)(2,1)}), bf16[16,7,128,128]{3,2,1,0:T(8,128)(2,1)}, u32[]{:S(2)}, u32[]{:S(2)}) async-start(bf16[16,7,128,128]{3,2,1,0:T(8,128)(2,1)} %copy-done), calls=%async_computation.3 | async-start | bytes 7340032 | tf_op jit(solution)/shard_map/all_to_all | solution.py:30
  238.4 8.3 %attend.4 = bf16[512,256]{1,0:T(8,128)(2,1)S(1)} custom-call(s32[1]{0:T(128)} %bitcast.pos_ref, bf16[2,4,512,128]{3,2,1,0:T(8,128)(2,1)S(1)} %copy-done.10, bf16[4,2,2,896,128]{4,3,2,1,0:T(8,128)(2,1)} %bitcast.35.k_ref.v_ref, bf16[4,2,2,896,128]{4,3,2,1,0:T(8,128)(2,1)} %bitcast.35.k_ref.v_ref, ...), custom_call_target="tpu_custom_call" | custom-call | flops 8589934592 | bytes 4194304 | tf_op jit(solution)/shard_map/attend/pallas_call | solution.py:216
  252.5 29.4 %all-gather.13.cloned.1.call-done = bf16[32,1,4,128,128]{4,3,2,1,0:T(8,128)(2,1)} async-done(((bf16[4,1,4,128,128]{4,3,2,1,0:T(8,128)(2,1)}), bf16[32,1,4,128,128]{4,3,2,1,0:T(8,128)(2,1)}) %all-gather.13.cloned.1.call-update) | async-done | bytes 4194320 | tf_op jit(solution)/shard_map/all_gather | solution.py:289
  287.6 11.7 %all-to-all-start.4 = ((bf16[16,7,128,128]{3,2,1,0:T(8,128)(2,1)}), bf16[16,7,128,128]{3,2,1,0:T(8,128)(2,1)}, u32[]{:S(2)}, u32[]{:S(2)}) async-start(bf16[16,7,128,128]{3,2,1,0:T(8,128)(2,1)} %copy-done.1), calls=%async_computation.4 | async-start | bytes 7340032 | tf_op jit(solution)/shard_map/all_to_all | solution.py:30
  299.4 8.4 %attend.5 = bf16[512,256]{1,0:T(8,128)(2,1)S(1)} custom-call(s32[1]{0:T(128)} %bitcast.pos_ref, bf16[2,4,512,128]{3,2,1,0:T(8,128)(2,1)S(1)} %copy-done.10, bf16[4,2,2,896,128]{4,3,2,1,0:T(8,128)(2,1)} %bitcast.37.k_ref.v_ref, bf16[4,2,2,896,128]{4,3,2,1,0:T(8,128)(2,1)} %bitcast.37.k_ref.v_ref, ...), custom_call_target="tpu_custom_call" | custom-call | flops 8589934592 | bytes 4194304 | tf_op jit(solution)/shard_map/attend/pallas_call | solution.py:216
  315.1 21.9 %all-gather.15.cloned.1.call-done = bf16[32,1,4,128,128]{4,3,2,1,0:T(8,128)(2,1)} async-done(((bf16[4,1,4,128,128]{4,3,2,1,0:T(8,128)(2,1)}), bf16[32,1,4,128,128]{4,3,2,1,0:T(8,128)(2,1)}) %all-gather.15.cloned.1.call-update) | async-done | bytes 4194320 | tf_op jit(solution)/shard_map/all_gather | solution.py:289
  344.6 4.5 %all-to-all-start.5 = ((bf16[16,7,128,128]{3,2,1,0:T(8,128)(2,1)}), bf16[16,7,128,128]{3,2,1,0:T(8,128)(2,1)}, u32[]{:S(2)}, u32[]{:S(2)}) async-start(bf16[16,7,128,128]{3,2,1,0:T(8,128)(2,1)} %copy-done.3), calls=%async_computation.5 | async-start | bytes 7340032 | tf_op jit(solution)/shard_map/all_to_all | solution.py:30
  349.2 8.4 %attend.6 = bf16[512,256]{1,0:T(8,128)(2,1)S(1)} custom-call(s32[1]{0:T(128)} %bitcast.pos_ref, bf16[2,4,512,128]{3,2,1,0:T(8,128)(2,1)S(1)} %copy-done.10, bf16[4,2,2,896,128]{4,3,2,1,0:T(8,128)(2,1)} %bitcast.39.k_ref.v_ref, bf16[4,2,2,896,128]{4,3,2,1,0:T(8,128)(2,1)} %bitcast.39.k_ref.v_ref, ...), custom_call_target="tpu_custom_call" | custom-call | flops 8589934592 | bytes 4194304 | tf_op jit(solution)/shard_map/attend/pallas_call | solution.py:216
  357.6 5.1 %collective-permute-start.16 = (bf16[256,256]{1,0:T(8,128)(2,1)S(1)}, bf16[256,256]{1,0:T(8,128)(2,1)S(1)}, u32[]{:S(2)}, u32[]{:S(2)}) collective-permute-start(bf16[256,256]{1,0:T(8,128)(2,1)S(1)} %constant_dynamic-slice_fusion.1), channel_id=1, source_target_pairs={{0,1},{1,0},{2,3},{3,2},{4,5},{5,4},{6,7},{7,6},{8,9},{9,8},{10,11... | collective-permute-start | bytes 393224 | tf_op jit(solution)/shard_map/ppermute | solution.py:300
  365.7 26.8 %all-to-all-done.5 = bf16[16,7,128,128]{3,2,1,0:T(8,128)(2,1)} async-done(((bf16[16,7,128,128]{3,2,1,0:T(8,128)(2,1)}), bf16[16,7,128,128]{3,2,1,0:T(8,128)(2,1)}, u32[]{:S(2)}, u32[]{:S(2)}) %all-to-all-start.5) | async-done | bytes 3670048 | tf_op jit(solution)/shard_map/all_to_all | solution.py:30
  392.5 8.2 %attend.7 = bf16[512,256]{1,0:T(8,128)(2,1)S(1)} custom-call(s32[1]{0:T(128)} %bitcast.pos_ref, bf16[2,4,512,128]{3,2,1,0:T(8,128)(2,1)S(1)} %copy-done.10, bf16[4,2,2,896,128]{4,3,2,1,0:T(8,128)(2,1)} %bitcast.41.k_ref.v_ref, bf16[4,2,2,896,128]{4,3,2,1,0:T(8,128)(2,1)} %bitcast.41.k_ref.v_ref, ...), custom_call_target="tpu_custom_call" | custom-call | flops 8589934592 | bytes 4194304 | tf_op jit(solution)/shard_map/attend/pallas_call | solution.py:216
  402.6 4.4 %collective-permute-start.17 = (bf16[256,256]{1,0:T(8,128)(2,1)S(1)}, bf16[256,256]{1,0:T(8,128)(2,1)S(1)}, u32[]{:S(2)}, u32[]{:S(2)}) collective-permute-start(bf16[256,256]{1,0:T(8,128)(2,1)S(1)} %constant_dynamic-slice_fusion), channel_id=1, source_target_pairs={{0,1},{1,0},{2,3},{3,2},{4,5},{5,4},{6,7},{7,6},{8,9},{9,8},{10,11... | collective-permute-start | bytes 393224 | tf_op jit(solution)/shard_map/ppermute | solution.py:300
  (130 shorter events, 94.4 us)
Async XLA Ops:
  13.2 42.7 %all-to-all-start = ((bf16[16,400,128]{2,1,0:T(8,128)(2,1)}), bf16[16,400,128]{2,1,0:T(8,128)(2,1)S(1)}, u32[]{:S(2)}, u32[]{:S(2)}) async-start(bf16[16,400,128]{2,1,0:T(8,128)(2,1)} %pack.2), calls=%async_computation | async-start | bytes 3276800 | tf_op jit(solution)/shard_map/all_to_all | solution.py:30
  22.4 140.1 %all-gather.9.cloned.1.call-start = ((), (), s32[]{:S(2)}) async-start(), calls=%async_computation.6 | async-start | bytes 4718592 | tf_op jit(solution)/shard_map/all_gather | solution.py:289
  60.1 6.2 %collective-permute-start.5 = (bf16[1,4,128,128]{3,2,1,0:T(8,128)(2,1)S(1)}, bf16[1,4,128,128]{3,2,1,0:T(8,128)(2,1)S(1)}, u32[]{:S(2)}, u32[]{:S(2)}) collective-permute-start(bf16[1,4,128,128]{3,2,1,0:T(8,128)(2,1)S(1)} %get-tuple-element.36), channel_id=1, source_target_pairs={{0,128},{64,192},{128,0},{192,64},{1,129},{65,193},{129,1},{193,65... | collective-permute-start | bytes 393224 | tf_op jit(solution)/shard_map/ppermute | solution.py:39
  62.5 5.2 %collective-permute-start.6 = (bf16[1,4,128,128]{3,2,1,0:T(8,128)(2,1)S(1)}, bf16[1,4,128,128]{3,2,1,0:T(8,128)(2,1)S(1)}, u32[]{:S(2)}, u32[]{:S(2)}) collective-permute-start(bf16[1,4,128,128]{3,2,1,0:T(8,128)(2,1)S(1)} %get-tuple-element.35), channel_id=1, source_target_pairs={{0,192},{64,128},{128,64},{192,0},{1,193},{65,129},{129,65},{193,1... | collective-permute-start | bytes 393224 | tf_op jit(solution)/shard_map/ppermute | solution.py:39
  70.2 61.2 %all-to-all-start.1 = ((bf16[16,384,128]{2,1,0:T(8,128)(2,1)}), bf16[16,384,128]{2,1,0:T(8,128)(2,1)S(1)}, u32[]{:S(2)}, u32[]{:S(2)}) async-start(bf16[16,384,128]{2,1,0:T(8,128)(2,1)} %pack.3), calls=%async_computation.1 | async-start | bytes 3145728 | tf_op jit(solution)/shard_map/all_to_all | solution.py:30
  81.6 145.0 %all-gather.11.cloned.1.call-start = ((), (), s32[]{:S(2)}) async-start(), calls=%async_computation.7 | async-start | bytes 4718592 | tf_op jit(solution)/shard_map/all_gather | solution.py:289
  87.2 20.1 %collective-permute-start = (bf16[4,512,128]{2,1,0:T(8,128)(2,1)}, bf16[4,512,128]{2,1,0:T(8,128)(2,1)}, u32[]{:S(2)}, u32[]{:S(2)}) collective-permute-start(bf16[4,512,128]{2,1,0:T(8,128)(2,1)} %get-tuple-element.33), channel_id=1, source_target_pairs={{0,2},{2,0},{1,3},{3,1},{4,6},{6,4},{5,7},{7,5},{8,10},{10,8},{9,1... | collective-permute-start | bytes 1572872 | tf_op jit(solution)/shard_map/ppermute | solution.py:275
  88.7 4.3 %collective-permute-start.2 = (s32[4,8]{1,0:T(4,128)S(1)}, s32[4,8]{1,0:T(4,128)S(1)}, u32[]{:S(2)}, u32[]{:S(2)}) collective-permute-start(s32[4,8]{1,0:T(4,128)S(1)} %bitcast.84), channel_id=1, source_target_pairs={{0,128},{64,192},{128,0},{192,64},{1,129},{65,193},{129,1},{193,65... | collective-permute-start | bytes 392 | tf_op jit(solution)/shard_map/ppermute | solution.py:39
  139.8 7.2 %collective-permute-start.7 = (bf16[3,4,128,128]{3,2,1,0:T(8,128)(2,1)}, bf16[3,4,128,128]{3,2,1,0:T(8,128)(2,1)S(1)}, u32[]{:S(2)}, u32[]{:S(2)}) collective-permute-start(bf16[3,4,128,128]{3,2,1,0:T(8,128)(2,1)} %get-tuple-element.31), channel_id=1, source_target_pairs={{0,64},{64,0},{128,192},{192,128},{1,65},{65,1},{129,193},{193,129... | collective-permute-start | bytes 1179656 | tf_op jit(solution)/shard_map/ppermute | solution.py:39
  139.9 13.1 %collective-permute-start.8 = (bf16[3,4,128,128]{3,2,1,0:T(8,128)(2,1)}, bf16[3,4,128,128]{3,2,1,0:T(8,128)(2,1)S(1)}, u32[]{:S(2)}, u32[]{:S(2)}) collective-permute-start(bf16[3,4,128,128]{3,2,1,0:T(8,128)(2,1)} %get-tuple-element.30), channel_id=1, source_target_pairs={{0,128},{64,192},{128,0},{192,64},{1,129},{65,193},{129,1},{193,65... | collective-permute-start | bytes 1179656 | tf_op jit(solution)/shard_map/ppermute | solution.py:39
  140.9 13.9 %collective-permute-start.9 = (bf16[3,4,128,128]{3,2,1,0:T(8,128)(2,1)}, bf16[3,4,128,128]{3,2,1,0:T(8,128)(2,1)S(1)}, u32[]{:S(2)}, u32[]{:S(2)}) collective-permute-start(bf16[3,4,128,128]{3,2,1,0:T(8,128)(2,1)} %get-tuple-element.29), channel_id=1, source_target_pairs={{0,192},{64,128},{128,64},{192,0},{1,193},{65,129},{129,65},{193,1... | collective-permute-start | bytes 1179656 | tf_op jit(solution)/shard_map/ppermute | solution.py:39
  143.9 11.1 %collective-permute-start.10 = (bf16[4,4,128,128]{3,2,1,0:T(8,128)(2,1)S(1)}, bf16[4,4,128,128]{3,2,1,0:T(8,128)(2,1)S(1)}, u32[]{:S(2)}, u32[]{:S(2)}) collective-permute-start(bf16[4,4,128,128]{3,2,1,0:T(8,128)(2,1)S(1)} %get-tuple-element.22), channel_id=1, source_target_pairs={{0,2},{2,0},{4,6},{6,4},{1,3},{3,1},{5,7},{7,5},{8,10},{10,8},{12,... | collective-permute-start | bytes 1572872 | tf_op jit(solution)/shard_map/ppermute | solution.py:39
  144.3 16.0 %collective-permute-start.11 = (bf16[4,4,128,128]{3,2,1,0:T(8,128)(2,1)S(1)}, bf16[4,4,128,128]{3,2,1,0:T(8,128)(2,1)S(1)}, u32[]{:S(2)}, u32[]{:S(2)}) collective-permute-start(bf16[4,4,128,128]{3,2,1,0:T(8,128)(2,1)S(1)} %get-tuple-element.23), channel_id=1, source_target_pairs={{0,4},{2,6},{4,0},{6,2},{1,5},{3,7},{5,1},{7,3},{8,12},{10,14},{12... | collective-permute-start | bytes 1572872 | tf_op jit(solution)/shard_map/ppermute | solution.py:39
  147.1 13.1 %collective-permute-start.12 = (bf16[4,4,128,128]{3,2,1,0:T(8,128)(2,1)S(1)}, bf16[4,4,128,128]{3,2,1,0:T(8,128)(2,1)S(1)}, u32[]{:S(2)}, u32[]{:S(2)}) collective-permute-start(bf16[4,4,128,128]{3,2,1,0:T(8,128)(2,1)S(1)} %get-tuple-element.24), channel_id=1, source_target_pairs={{0,6},{2,4},{4,2},{6,0},{1,7},{3,5},{5,3},{7,1},{8,14},{10,12},{12... | collective-permute-start | bytes 1572872 | tf_op jit(solution)/shard_map/ppermute | solution.py:39
  161.7 120.1 %all-gather.13.cloned.1.call-start = ((), (), s32[]{:S(2)}) async-start(), calls=%async_computation.8 | async-start | bytes 4718592 | tf_op jit(solution)/shard_map/all_gather | solution.py:289
  167.3 64.1 %all-to-all-start.2 = ((bf16[16,7,128,128]{3,2,1,0:T(8,128)(2,1)}), bf16[16,7,128,128]{3,2,1,0:T(8,128)(2,1)}, u32[]{:S(2)}, u32[]{:S(2)}) async-start(bf16[16,7,128,128]{3,2,1,0:T(8,128)(2,1)} %copy-done.2), calls=%async_computation.2 | async-start | bytes 7340032 | tf_op jit(solution)/shard_map/all_to_all | solution.py:30
  176.6 160.4 %all-gather.15.cloned.1.call-start = ((), (), s32[]{:S(2)}) async-start(), calls=%async_computation.9 | async-start | bytes 4718592 | tf_op jit(solution)/shard_map/all_gather | solution.py:289
  176.6 72.8 %collective-permute-start.14 = (bf16[1024,2048]{1,0:T(8,128)(2,1)}, bf16[1024,2048]{1,0:T(8,128)(2,1)}, u32[]{:S(2)}, u32[]{:S(2)}) collective-permute-start(bf16[1024,2048]{1,0:T(8,128)(2,1)} %param.11), channel_id=1, source_target_pairs={{0,1},{1,0},{2,3},{3,2},{4,5},{5,4},{6,7},{7,6},{8,9},{9,8},{10,11... | collective-permute-start | bytes 12582920 | tf_op jit(solution)/shard_map/ppermute | solution.py:249
  231.4 56.3 %all-to-all-start.3 = ((bf16[16,7,128,128]{3,2,1,0:T(8,128)(2,1)}), bf16[16,7,128,128]{3,2,1,0:T(8,128)(2,1)}, u32[]{:S(2)}, u32[]{:S(2)}) async-start(bf16[16,7,128,128]{3,2,1,0:T(8,128)(2,1)} %copy-done), calls=%async_computation.3 | async-start | bytes 7340032 | tf_op jit(solution)/shard_map/all_to_all | solution.py:30
  287.6 57.0 %all-to-all-start.4 = ((bf16[16,7,128,128]{3,2,1,0:T(8,128)(2,1)}), bf16[16,7,128,128]{3,2,1,0:T(8,128)(2,1)}, u32[]{:S(2)}, u32[]{:S(2)}) async-start(bf16[16,7,128,128]{3,2,1,0:T(8,128)(2,1)} %copy-done.1), calls=%async_computation.4 | async-start | bytes 7340032 | tf_op jit(solution)/shard_map/all_to_all | solution.py:30
  307.8 4.2 collective-permute-start.15
  344.6 47.9 %all-to-all-start.5 = ((bf16[16,7,128,128]{3,2,1,0:T(8,128)(2,1)}), bf16[16,7,128,128]{3,2,1,0:T(8,128)(2,1)}, u32[]{:S(2)}, u32[]{:S(2)}) async-start(bf16[16,7,128,128]{3,2,1,0:T(8,128)(2,1)} %copy-done.3), calls=%async_computation.5 | async-start | bytes 7340032 | tf_op jit(solution)/shard_map/all_to_all | solution.py:30
  357.6 49.5 %collective-permute-start.16 = (bf16[256,256]{1,0:T(8,128)(2,1)S(1)}, bf16[256,256]{1,0:T(8,128)(2,1)S(1)}, u32[]{:S(2)}, u32[]{:S(2)}) collective-permute-start(bf16[256,256]{1,0:T(8,128)(2,1)S(1)} %constant_dynamic-slice_fusion.1), channel_id=1, source_target_pairs={{0,1},{1,0},{2,3},{3,2},{4,5},{5,4},{6,7},{7,6},{8,9},{9,8},{10,11... | collective-permute-start | bytes 393224 | tf_op jit(solution)/shard_map/ppermute | solution.py:300
  402.6 6.2 %collective-permute-start.17 = (bf16[256,256]{1,0:T(8,128)(2,1)S(1)}, bf16[256,256]{1,0:T(8,128)(2,1)S(1)}, u32[]{:S(2)}, u32[]{:S(2)}) collective-permute-start(bf16[256,256]{1,0:T(8,128)(2,1)S(1)} %constant_dynamic-slice_fusion), channel_id=1, source_target_pairs={{0,1},{1,0},{2,3},{3,2},{4,5},{5,4},{6,7},{7,6},{8,9},{9,8},{10,11... | collective-permute-start | bytes 393224 | tf_op jit(solution)/shard_map/ppermute | solution.py:300
  (20 other events, 88.8 us)
Sparse Core Ops, SparseCore 0:
  68.7 87.4 all-gather.8
  161.8 64.7 all-gather.10
  228.4 53.4 all-gather.12
  283.5 53.4 all-gather.14

commit v4 on v3

--- a/solution.py
+++ b/solution.py
@@ -282,16 +282,15 @@
     ordered, _, _ = lax.optimization_barrier((ordered, lists, query))
     every = jnp.concatenate([lead_ordered, ordered], axis=1)
     own = [lax.dynamic_index_in_dim(every, pos ^ d, 2, False) for d in range(4)]
-    later, own = lax.optimization_barrier(
-        (swapped(ordered, "x"), swapped(own, ("yh", "yl")))
-    )
+    later = swapped(ordered, "x")
+    own = swapped(own, ("yh", "yl"))
     spreads += [later[:, c] for c in range(CHUNKS - LEAD)]
     held = [lax.all_gather(part, LINE, axis=0) for part in spreads]
 
     half = BLOCK // 2
     results = [jnp.zeros((half, out_weight.shape[1]), jnp.float32)]
     for c in range(CHUNKS):
-        ready = after(lists, *((results[c - 1],) if c > 1 else (later,)))
+        ready = after(lists, *((results[c - 1],) if c > 1 else (later, own)))
         got = exchange(select(ready, flip, held[c]), PLANE)
         got = got.reshape(4, 2, 2, (SEL - 1) * PART, HD)
         attended = attend(pos.reshape(1), query, got, own, c)

time: 421 us -> 419 us (level); the launches traced: 418 us -> 411 us
  waiting for transfers between devices: 215 us -> 191 us
  starting transfers between devices: 87.5 us -> 103 us
    all_gather x4, waiting for transfers between devices: 94.3 us -> 49.5 us  [body(): held = [lax.all_gather(part, LINE, axis=0) for part in spreads]]
    ppermute x12, waiting for transfers between devices: 22.3 us -> 38 us  [swapped(): lax.ppermute(pieces[d], axes, [(i, i ^ d) for i in range(4)])]
    ppermute x4, starting transfers between devices: 13 us -> 27.3 us  [body(): other = lax.ppermute(theirs, 'core', swap)]
    all_to_all x6, waiting for transfers between devices: 86 us -> 91.4 us  [exchange(): return lax.all_to_all(value, axes, split_axis=0, concat_axis=0, tiled=True)]
  transfers between devices with their start and end apart: 28 -> 28, of which waited for: 17 -> 19; matrix products, arithmetic and copies ran while one was open for 6% -> 6% of each run, Pallas kernels for 13% -> 14%
where the time goes in v4:
time: 419 us; the launch traced here: 411 us
  waiting for transfers between devices  191 us (46%)
  starting transfers between devices  103 us (25%)
  Pallas kernels  59.7 us (14%)
  local copies, waits for them, and re-layouts  19.2 us (5%)
  matrix products  18.6 us (4%)
  between operations  13.7 us (3%)
  other arithmetic  5.13 us (1%)
    all_to_all x6, waiting for transfers between devices, exchange(): return lax.all_to_all(value, axes, split_axis=0, concat_axis=0, tiled=True)  91.4 us
    all_to_all x6, starting transfers between devices, exchange(): return lax.all_to_all(value, axes, split_axis=0, concat_axis=0, tiled=True)  51.2 us
    all_gather x4, waiting for transfers between devices, body(): held = [lax.all_gather(part, LINE, axis=0) for part in spreads]  49.5 us
    ppermute x12, waiting for transfers between devices, swapped(): lax.ppermute(pieces[d], axes, [(i, i ^ d) for i in range(4)])  38 us
    pallas_call x4, Pallas kernels, attend(): pl.pallas_call(functools.partial(attend_kernel, scale=math.log2(math.e) /...  33.4 us
    ppermute x4, starting transfers between devices, body(): other = lax.ppermute(theirs, 'core', swap)  27.3 us
    ppermute x12, starting transfers between devices, swapped(): lax.ppermute(pieces[d], axes, [(i, i ^ d) for i in range(4)])  15.8 us
    unnamed x32, local copies, waits for them, and re-layouts  14.5 us
  transfers between devices with their start and end apart: 28, of which 19 were waited for; matrix products, arithmetic and copies ran while one was open for 6% of the time, Pallas kernels for 14%

profile of v4, /device:TPU:1, one launch (start us, length us, event | category | flops | bytes accessed | tf_op | source)
XLA Modules:
  0.0 410.5 jit_solution(3018193361755155552)
XLA Ops:
  13.2 9.2 %all-to-all-start = ((bf16[16,400,128]{2,1,0:T(8,128)(2,1)}), bf16[16,400,128]{2,1,0:T(8,128)(2,1)S(1)}, u32[]{:S(2)}, u32[]{:S(2)}) async-start(bf16[16,400,128]{2,1,0:T(8,128)(2,1)} %pack.2), calls=%async_computation | async-start | bytes 3276800 | tf_op jit(solution)/shard_map/all_to_all | solution.py:30
  22.4 33.4 %all-to-all-done = bf16[16,400,128]{2,1,0:T(8,128)(2,1)S(1)} async-done(((bf16[16,400,128]{2,1,0:T(8,128)(2,1)}), bf16[16,400,128]{2,1,0:T(8,128)(2,1)S(1)}, u32[]{:S(2)}, u32[]{:S(2)}) %all-to-all-start) | async-done | bytes 1638432 | tf_op jit(solution)/shard_map/all_to_all | solution.py:30
  70.2 11.4 %all-to-all-start.1 = ((bf16[16,384,128]{2,1,0:T(8,128)(2,1)}), bf16[16,384,128]{2,1,0:T(8,128)(2,1)S(1)}, u32[]{:S(2)}, u32[]{:S(2)}) async-start(bf16[16,384,128]{2,1,0:T(8,128)(2,1)} %pack.3), calls=%async_computation.1 | async-start | bytes 3145728 | tf_op jit(solution)/shard_map/all_to_all | solution.py:30
  95.5 11.8 %collective-permute-done = bf16[4,512,128]{2,1,0:T(8,128)(2,1)} collective-permute-done((bf16[4,512,128]{2,1,0:T(8,128)(2,1)}, bf16[4,512,128]{2,1,0:T(8,128)(2,1)}, u32[]{:S(2)}, u32[]{:S(2)}) %collective-permute-start) | collective-permute-done | bytes 524320 | tf_op jit(solution)/shard_map/ppermute | solution.py:275
  109.4 22.0 %all-to-all-done.1 = bf16[16,384,128]{2,1,0:T(8,128)(2,1)S(1)} async-done(((bf16[16,384,128]{2,1,0:T(8,128)(2,1)}), bf16[16,384,128]{2,1,0:T(8,128)(2,1)S(1)}, u32[]{:S(2)}, u32[]{:S(2)}) %all-to-all-start.1) | async-done | bytes 1572896 | tf_op jit(solution)/shard_map/all_to_all | solution.py:30
  146.1 5.9 %collective-permute-done.8 = bf16[3,4,128,128]{3,2,1,0:T(8,128)(2,1)S(1)} collective-permute-done((bf16[3,4,128,128]{3,2,1,0:T(8,128)(2,1)S(1)}, bf16[3,4,128,128]{3,2,1,0:T(8,128)(2,1)S(1)}, u32[]{:S(2)}, u32[]{:S(2)}) %collective-permute-start.8) | collective-permute-done | bytes 393248 | tf_op jit(solution)/shard_map/ppermute | solution.py:39
  164.1 7.3 %collective-permute-done.11 = bf16[4,4,128,128]{3,2,1,0:T(8,128)(2,1)S(1)} collective-permute-done((bf16[4,4,128,128]{3,2,1,0:T(8,128)(2,1)S(1)}, bf16[4,4,128,128]{3,2,1,0:T(8,128)(2,1)S(1)}, u32[]{:S(2)}, u32[]{:S(2)}) %collective-permute-start.11) | collective-permute-done | bytes 524320 | tf_op jit(solution)/shard_map/ppermute | solution.py:39
  171.4 8.5 %collective-permute-done.12 = bf16[4,4,128,128]{3,2,1,0:T(8,128)(2,1)S(1)} collective-permute-done((bf16[4,4,128,128]{3,2,1,0:T(8,128)(2,1)S(1)}, bf16[4,4,128,128]{3,2,1,0:T(8,128)(2,1)S(1)}, u32[]{:S(2)}, u32[]{:S(2)}) %collective-permute-start.12) | collective-permute-done | bytes 524320 | tf_op jit(solution)/shard_map/ppermute | solution.py:39
  189.9 6.9 %collective-permute-start.14 = (bf16[1024,2048]{1,0:T(8,128)(2,1)}, bf16[1024,2048]{1,0:T(8,128)(2,1)}, u32[]{:S(2)}, u32[]{:S(2)}) collective-permute-start(bf16[1024,2048]{1,0:T(8,128)(2,1)} %param.11), channel_id=1, source_target_pairs={{0,1},{1,0},{2,3},{3,2},{4,5},{5,4},{6,7},{7,6},{8,9},{9,8},{10,11... | collective-permute-start | bytes 12582920 | tf_op jit(solution)/shard_map/ppermute | solution.py:249
  196.8 20.7 %all-gather.11.cloned.1.call-done = bf16[32,1,4,128,128]{4,3,2,1,0:T(8,128)(2,1)} async-done(((bf16[4,1,4,128,128]{4,3,2,1,0:T(8,128)(2,1)}), bf16[32,1,4,128,128]{4,3,2,1,0:T(8,128)(2,1)}) %all-gather.11.cloned.1.call-update) | async-done | bytes 4194320 | tf_op jit(solution)/shard_map/all_gather | solution.py:288
  222.7 7.0 %all-to-all-done.2 = bf16[16,7,128,128]{3,2,1,0:T(8,128)(2,1)} async-done(((bf16[16,7,128,128]{3,2,1,0:T(8,128)(2,1)}), bf16[16,7,128,128]{3,2,1,0:T(8,128)(2,1)}, u32[]{:S(2)}, u32[]{:S(2)}) %all-to-all-start.2) | async-done | bytes 3670048 | tf_op jit(solution)/shard_map/all_to_all | solution.py:30
  229.7 10.2 %all-to-all-start.3 = ((bf16[16,7,128,128]{3,2,1,0:T(8,128)(2,1)}), bf16[16,7,128,128]{3,2,1,0:T(8,128)(2,1)}, u32[]{:S(2)}, u32[]{:S(2)}) async-start(bf16[16,7,128,128]{3,2,1,0:T(8,128)(2,1)} %copy-done), calls=%async_computation.3 | async-start | bytes 7340032 | tf_op jit(solution)/shard_map/all_to_all | solution.py:30
  239.9 8.3 %attend.4 = bf16[512,256]{1,0:T(8,128)(2,1)S(1)} custom-call(s32[1]{0:T(128)} %bitcast.pos_ref, bf16[2,4,512,128]{3,2,1,0:T(8,128)(2,1)S(1)} %copy-done.10, bf16[4,2,2,896,128]{4,3,2,1,0:T(8,128)(2,1)} %bitcast.35.k_ref.v_ref, bf16[4,2,2,896,128]{4,3,2,1,0:T(8,128)(2,1)} %bitcast.35.k_ref.v_ref, ...), custom_call_target="tpu_custom_call" | custom-call | flops 8589934592 | bytes 4194304 | tf_op jit(solution)/shard_map/attend/pallas_call | solution.py:216
  248.2 7.7 %collective-permute-start.13 = (bf16[256,256]{1,0:T(8,128)(2,1)S(1)}, bf16[256,256]{1,0:T(8,128)(2,1)S(1)}, u32[]{:S(2)}, u32[]{:S(2)}) collective-permute-start(bf16[256,256]{1,0:T(8,128)(2,1)S(1)} %constant_dynamic-slice_fusion.3), channel_id=1, source_target_pairs={{0,1},{1,0},{2,3},{3,2},{4,5},{5,4},{6,7},{7,6},{8,9},{9,8},{10,11... | collective-permute-start | bytes 393224 | tf_op jit(solution)/shard_map/ppermute | solution.py:299
  260.7 12.1 %all-gather.13.cloned.1.call-done = bf16[32,1,4,128,128]{4,3,2,1,0:T(8,128)(2,1)} async-done(((bf16[4,1,4,128,128]{4,3,2,1,0:T(8,128)(2,1)}), bf16[32,1,4,128,128]{4,3,2,1,0:T(8,128)(2,1)}) %all-gather.13.cloned.1.call-update) | async-done | bytes 4194320 | tf_op jit(solution)/shard_map/all_gather | solution.py:288
  279.1 9.6 %all-to-all-start.4 = ((bf16[16,7,128,128]{3,2,1,0:T(8,128)(2,1)}), bf16[16,7,128,128]{3,2,1,0:T(8,128)(2,1)}, u32[]{:S(2)}, u32[]{:S(2)}) async-start(bf16[16,7,128,128]{3,2,1,0:T(8,128)(2,1)} %copy-done.1), calls=%async_computation.4 | async-start | bytes 7340032 | tf_op jit(solution)/shard_map/all_to_all | solution.py:30
  288.7 8.4 %attend.5 = bf16[512,256]{1,0:T(8,128)(2,1)S(1)} custom-call(s32[1]{0:T(128)} %bitcast.pos_ref, bf16[2,4,512,128]{3,2,1,0:T(8,128)(2,1)S(1)} %copy-done.10, bf16[4,2,2,896,128]{4,3,2,1,0:T(8,128)(2,1)} %bitcast.37.k_ref.v_ref, bf16[4,2,2,896,128]{4,3,2,1,0:T(8,128)(2,1)} %bitcast.37.k_ref.v_ref, ...), custom_call_target="tpu_custom_call" | custom-call | flops 8589934592 | bytes 4194304 | tf_op jit(solution)/shard_map/attend/pallas_call | solution.py:216
  297.1 9.2 %collective-permute-start.15 = (bf16[256,256]{1,0:T(8,128)(2,1)S(1)}, bf16[256,256]{1,0:T(8,128)(2,1)S(1)}, u32[]{:S(2)}, u32[]{:S(2)}) collective-permute-start(bf16[256,256]{1,0:T(8,128)(2,1)S(1)} %constant_dynamic-slice_fusion.2), channel_id=1, source_target_pairs={{0,1},{1,0},{2,3},{3,2},{4,5},{5,4},{6,7},{7,6},{8,9},{9,8},{10,11... | collective-permute-start | bytes 393224 | tf_op jit(solution)/shard_map/ppermute | solution.py:299
  311.1 16.8 %all-gather.15.cloned.1.call-done = bf16[32,1,4,128,128]{4,3,2,1,0:T(8,128)(2,1)} async-done(((bf16[4,1,4,128,128]{4,3,2,1,0:T(8,128)(2,1)}), bf16[32,1,4,128,128]{4,3,2,1,0:T(8,128)(2,1)}) %all-gather.15.cloned.1.call-update) | async-done | bytes 4194320 | tf_op jit(solution)/shard_map/all_gather | solution.py:288
  333.2 6.3 %all-to-all-start.5 = ((bf16[16,7,128,128]{3,2,1,0:T(8,128)(2,1)}), bf16[16,7,128,128]{3,2,1,0:T(8,128)(2,1)}, u32[]{:S(2)}, u32[]{:S(2)}) async-start(bf16[16,7,128,128]{3,2,1,0:T(8,128)(2,1)} %copy-done.3), calls=%async_computation.5 | async-start | bytes 7340032 | tf_op jit(solution)/shard_map/all_to_all | solution.py:30
  339.6 8.4 %attend.6 = bf16[512,256]{1,0:T(8,128)(2,1)S(1)} custom-call(s32[1]{0:T(128)} %bitcast.pos_ref, bf16[2,4,512,128]{3,2,1,0:T(8,128)(2,1)S(1)} %copy-done.10, bf16[4,2,2,896,128]{4,3,2,1,0:T(8,128)(2,1)} %bitcast.39.k_ref.v_ref, bf16[4,2,2,896,128]{4,3,2,1,0:T(8,128)(2,1)} %bitcast.39.k_ref.v_ref, ...), custom_call_target="tpu_custom_call" | custom-call | flops 8589934592 | bytes 4194304 | tf_op jit(solution)/shard_map/attend/pallas_call | solution.py:216
  353.7 28.1 %all-to-all-done.5 = bf16[16,7,128,128]{3,2,1,0:T(8,128)(2,1)} async-done(((bf16[16,7,128,128]{3,2,1,0:T(8,128)(2,1)}), bf16[16,7,128,128]{3,2,1,0:T(8,128)(2,1)}, u32[]{:S(2)}, u32[]{:S(2)}) %all-to-all-start.5) | async-done | bytes 3670048 | tf_op jit(solution)/shard_map/all_to_all | solution.py:30
  381.7 8.2 %attend.7 = bf16[512,256]{1,0:T(8,128)(2,1)S(1)} custom-call(s32[1]{0:T(128)} %bitcast.pos_ref, bf16[2,4,512,128]{3,2,1,0:T(8,128)(2,1)S(1)} %copy-done.10, bf16[4,2,2,896,128]{4,3,2,1,0:T(8,128)(2,1)} %bitcast.41.k_ref.v_ref, bf16[4,2,2,896,128]{4,3,2,1,0:T(8,128)(2,1)} %bitcast.41.k_ref.v_ref, ...), custom_call_target="tpu_custom_call" | custom-call | flops 8589934592 | bytes 4194304 | tf_op jit(solution)/shard_map/attend/pallas_call | solution.py:216
  391.9 7.7 %collective-permute-start.17 = (bf16[256,256]{1,0:T(8,128)(2,1)S(1)}, bf16[256,256]{1,0:T(8,128)(2,1)S(1)}, u32[]{:S(2)}, u32[]{:S(2)}) collective-permute-start(bf16[256,256]{1,0:T(8,128)(2,1)S(1)} %constant_dynamic-slice_fusion), channel_id=1, source_target_pairs={{0,1},{1,0},{2,3},{3,2},{4,5},{5,4},{6,7},{7,6},{8,9},{9,8},{10,11... | collective-permute-start | bytes 393224 | tf_op jit(solution)/shard_map/ppermute | solution.py:299
  (130 shorter events, 111.8 us)
Async XLA Ops:
  13.2 42.7 %all-to-all-start = ((bf16[16,400,128]{2,1,0:T(8,128)(2,1)}), bf16[16,400,128]{2,1,0:T(8,128)(2,1)S(1)}, u32[]{:S(2)}, u32[]{:S(2)}) async-start(bf16[16,400,128]{2,1,0:T(8,128)(2,1)} %pack.2), calls=%async_computation | async-start | bytes 3276800 | tf_op jit(solution)/shard_map/all_to_all | solution.py:30
  22.4 157.8 %all-gather.9.cloned.1.call-start = ((), (), s32[]{:S(2)}) async-start(), calls=%async_computation.6 | async-start | bytes 4718592 | tf_op jit(solution)/shard_map/all_gather | solution.py:288
  60.1 6.2 %collective-permute-start.5 = (bf16[1,4,128,128]{3,2,1,0:T(8,128)(2,1)S(1)}, bf16[1,4,128,128]{3,2,1,0:T(8,128)(2,1)S(1)}, u32[]{:S(2)}, u32[]{:S(2)}) collective-permute-start(bf16[1,4,128,128]{3,2,1,0:T(8,128)(2,1)S(1)} %get-tuple-element.32), channel_id=1, source_target_pairs={{0,128},{64,192},{128,0},{192,64},{1,129},{65,193},{129,1},{193,65... | collective-permute-start | bytes 393224 | tf_op jit(solution)/shard_map/ppermute | solution.py:39
  62.5 5.2 %collective-permute-start.6 = (bf16[1,4,128,128]{3,2,1,0:T(8,128)(2,1)S(1)}, bf16[1,4,128,128]{3,2,1,0:T(8,128)(2,1)S(1)}, u32[]{:S(2)}, u32[]{:S(2)}) collective-permute-start(bf16[1,4,128,128]{3,2,1,0:T(8,128)(2,1)S(1)} %get-tuple-element.31), channel_id=1, source_target_pairs={{0,192},{64,128},{128,64},{192,0},{1,193},{65,129},{129,65},{193,1... | collective-permute-start | bytes 393224 | tf_op jit(solution)/shard_map/ppermute | solution.py:39
  70.2 61.2 %all-to-all-start.1 = ((bf16[16,384,128]{2,1,0:T(8,128)(2,1)}), bf16[16,384,128]{2,1,0:T(8,128)(2,1)S(1)}, u32[]{:S(2)}, u32[]{:S(2)}) async-start(bf16[16,384,128]{2,1,0:T(8,128)(2,1)} %pack.3), calls=%async_computation.1 | async-start | bytes 3145728 | tf_op jit(solution)/shard_map/all_to_all | solution.py:30
  81.6 135.9 %all-gather.11.cloned.1.call-start = ((), (), s32[]{:S(2)}) async-start(), calls=%async_computation.7 | async-start | bytes 4718592 | tf_op jit(solution)/shard_map/all_gather | solution.py:288
  87.2 20.1 %collective-permute-start = (bf16[4,512,128]{2,1,0:T(8,128)(2,1)}, bf16[4,512,128]{2,1,0:T(8,128)(2,1)}, u32[]{:S(2)}, u32[]{:S(2)}) collective-permute-start(bf16[4,512,128]{2,1,0:T(8,128)(2,1)} %get-tuple-element.29), channel_id=1, source_target_pairs={{0,2},{2,0},{1,3},{3,1},{4,6},{6,4},{5,7},{7,5},{8,10},{10,8},{9,1... | collective-permute-start | bytes 1572872 | tf_op jit(solution)/shard_map/ppermute | solution.py:275
  138.9 7.1 %collective-permute-start.7 = (bf16[3,4,128,128]{3,2,1,0:T(8,128)(2,1)S(1)}, bf16[3,4,128,128]{3,2,1,0:T(8,128)(2,1)S(1)}, u32[]{:S(2)}, u32[]{:S(2)}) collective-permute-start(bf16[3,4,128,128]{3,2,1,0:T(8,128)(2,1)S(1)} %get-tuple-element.27), channel_id=1, source_target_pairs={{0,64},{64,0},{128,192},{192,128},{1,65},{65,1},{129,193},{193,129... | collective-permute-start | bytes 1179656 | tf_op jit(solution)/shard_map/ppermute | solution.py:39
  139.0 12.9 %collective-permute-start.8 = (bf16[3,4,128,128]{3,2,1,0:T(8,128)(2,1)S(1)}, bf16[3,4,128,128]{3,2,1,0:T(8,128)(2,1)S(1)}, u32[]{:S(2)}, u32[]{:S(2)}) collective-permute-start(bf16[3,4,128,128]{3,2,1,0:T(8,128)(2,1)S(1)} %get-tuple-element.26), channel_id=1, source_target_pairs={{0,128},{64,192},{128,0},{192,64},{1,129},{65,193},{129,1},{193,65... | collective-permute-start | bytes 1179656 | tf_op jit(solution)/shard_map/ppermute | solution.py:39
  140.1 13.6 %collective-permute-start.9 = (bf16[3,4,128,128]{3,2,1,0:T(8,128)(2,1)S(1)}, bf16[3,4,128,128]{3,2,1,0:T(8,128)(2,1)S(1)}, u32[]{:S(2)}, u32[]{:S(2)}) collective-permute-start(bf16[3,4,128,128]{3,2,1,0:T(8,128)(2,1)S(1)} %get-tuple-element.25), channel_id=1, source_target_pairs={{0,192},{64,128},{128,64},{192,0},{1,193},{65,129},{129,65},{193,1... | collective-permute-start | bytes 1179656 | tf_op jit(solution)/shard_map/ppermute | solution.py:39
  155.1 117.7 %all-gather.13.cloned.1.call-start = ((), (), s32[]{:S(2)}) async-start(), calls=%async_computation.8 | async-start | bytes 4718592 | tf_op jit(solution)/shard_map/all_gather | solution.py:288
  156.0 8.1 %collective-permute-start.10 = (bf16[4,4,128,128]{3,2,1,0:T(8,128)(2,1)S(1)}, bf16[4,4,128,128]{3,2,1,0:T(8,128)(2,1)S(1)}, u32[]{:S(2)}, u32[]{:S(2)}) collective-permute-start(bf16[4,4,128,128]{3,2,1,0:T(8,128)(2,1)S(1)} %get-tuple-element.18), channel_id=1, source_target_pairs={{0,2},{2,0},{4,6},{6,4},{1,3},{3,1},{5,7},{7,5},{8,10},{10,8},{12,... | collective-permute-start | bytes 1572872 | tf_op jit(solution)/shard_map/ppermute | solution.py:39
  156.5 14.9 %collective-permute-start.11 = (bf16[4,4,128,128]{3,2,1,0:T(8,128)(2,1)S(1)}, bf16[4,4,128,128]{3,2,1,0:T(8,128)(2,1)S(1)}, u32[]{:S(2)}, u32[]{:S(2)}) collective-permute-start(bf16[4,4,128,128]{3,2,1,0:T(8,128)(2,1)S(1)} %get-tuple-element.19), channel_id=1, source_target_pairs={{0,4},{2,6},{4,0},{6,2},{1,5},{3,7},{5,1},{7,3},{8,12},{10,14},{12... | collective-permute-start | bytes 1572872 | tf_op jit(solution)/shard_map/ppermute | solution.py:39
  156.5 23.4 %collective-permute-start.12 = (bf16[4,4,128,128]{3,2,1,0:T(8,128)(2,1)S(1)}, bf16[4,4,128,128]{3,2,1,0:T(8,128)(2,1)S(1)}, u32[]{:S(2)}, u32[]{:S(2)}) collective-permute-start(bf16[4,4,128,128]{3,2,1,0:T(8,128)(2,1)S(1)} %get-tuple-element.20), channel_id=1, source_target_pairs={{0,6},{2,4},{4,2},{6,0},{1,7},{3,5},{5,3},{7,1},{8,14},{10,12},{12... | collective-permute-start | bytes 1572872 | tf_op jit(solution)/shard_map/ppermute | solution.py:39
  185.3 44.4 %all-to-all-start.2 = ((bf16[16,7,128,128]{3,2,1,0:T(8,128)(2,1)}), bf16[16,7,128,128]{3,2,1,0:T(8,128)(2,1)}, u32[]{:S(2)}, u32[]{:S(2)}) async-start(bf16[16,7,128,128]{3,2,1,0:T(8,128)(2,1)} %copy-done.2), calls=%async_computation.2 | async-start | bytes 7340032 | tf_op jit(solution)/shard_map/all_to_all | solution.py:30
  189.8 138.0 %all-gather.15.cloned.1.call-start = ((), (), s32[]{:S(2)}) async-start(), calls=%async_computation.9 | async-start | bytes 4718592 | tf_op jit(solution)/shard_map/all_gather | solution.py:288
  189.9 67.8 %collective-permute-start.14 = (bf16[1024,2048]{1,0:T(8,128)(2,1)}, bf16[1024,2048]{1,0:T(8,128)(2,1)}, u32[]{:S(2)}, u32[]{:S(2)}) collective-permute-start(bf16[1024,2048]{1,0:T(8,128)(2,1)} %param.11), channel_id=1, source_target_pairs={{0,1},{1,0},{2,3},{3,2},{4,5},{5,4},{6,7},{7,6},{8,9},{9,8},{10,11... | collective-permute-start | bytes 12582920 | tf_op jit(solution)/shard_map/ppermute | solution.py:249
  229.7 49.4 %all-to-all-start.3 = ((bf16[16,7,128,128]{3,2,1,0:T(8,128)(2,1)}), bf16[16,7,128,128]{3,2,1,0:T(8,128)(2,1)}, u32[]{:S(2)}, u32[]{:S(2)}) async-start(bf16[16,7,128,128]{3,2,1,0:T(8,128)(2,1)} %copy-done), calls=%async_computation.3 | async-start | bytes 7340032 | tf_op jit(solution)/shard_map/all_to_all | solution.py:30
  248.2 9.4 %collective-permute-start.13 = (bf16[256,256]{1,0:T(8,128)(2,1)S(1)}, bf16[256,256]{1,0:T(8,128)(2,1)S(1)}, u32[]{:S(2)}, u32[]{:S(2)}) collective-permute-start(bf16[256,256]{1,0:T(8,128)(2,1)S(1)} %constant_dynamic-slice_fusion.3), channel_id=1, source_target_pairs={{0,1},{1,0},{2,3},{3,2},{4,5},{5,4},{6,7},{7,6},{8,9},{9,8},{10,11... | collective-permute-start | bytes 393224 | tf_op jit(solution)/shard_map/ppermute | solution.py:299
  279.1 54.2 %all-to-all-start.4 = ((bf16[16,7,128,128]{3,2,1,0:T(8,128)(2,1)}), bf16[16,7,128,128]{3,2,1,0:T(8,128)(2,1)}, u32[]{:S(2)}, u32[]{:S(2)}) async-start(bf16[16,7,128,128]{3,2,1,0:T(8,128)(2,1)} %copy-done.1), calls=%async_computation.4 | async-start | bytes 7340032 | tf_op jit(solution)/shard_map/all_to_all | solution.py:30
  297.1 10.9 %collective-permute-start.15 = (bf16[256,256]{1,0:T(8,128)(2,1)S(1)}, bf16[256,256]{1,0:T(8,128)(2,1)S(1)}, u32[]{:S(2)}, u32[]{:S(2)}) collective-permute-start(bf16[256,256]{1,0:T(8,128)(2,1)S(1)} %constant_dynamic-slice_fusion.2), channel_id=1, source_target_pairs={{0,1},{1,0},{2,3},{3,2},{4,5},{5,4},{6,7},{7,6},{8,9},{9,8},{10,11... | collective-permute-start | bytes 393224 | tf_op jit(solution)/shard_map/ppermute | solution.py:299
  333.2 48.5 %all-to-all-start.5 = ((bf16[16,7,128,128]{3,2,1,0:T(8,128)(2,1)}), bf16[16,7,128,128]{3,2,1,0:T(8,128)(2,1)}, u32[]{:S(2)}, u32[]{:S(2)}) async-start(bf16[16,7,128,128]{3,2,1,0:T(8,128)(2,1)} %copy-done.3), calls=%async_computation.5 | async-start | bytes 7340032 | tf_op jit(solution)/shard_map/all_to_all | solution.py:30
  348.0 51.6 %collective-permute-start.16 = (bf16[256,256]{1,0:T(8,128)(2,1)S(1)}, bf16[256,256]{1,0:T(8,128)(2,1)S(1)}, u32[]{:S(2)}, u32[]{:S(2)}) collective-permute-start(bf16[256,256]{1,0:T(8,128)(2,1)S(1)} %constant_dynamic-slice_fusion.1), channel_id=1, source_target_pairs={{0,1},{1,0},{2,3},{3,2},{4,5},{5,4},{6,7},{7,6},{8,9},{9,8},{10,11... | collective-permute-start | bytes 393224 | tf_op jit(solution)/shard_map/ppermute | solution.py:299
  391.9 9.5 %collective-permute-start.17 = (bf16[256,256]{1,0:T(8,128)(2,1)S(1)}, bf16[256,256]{1,0:T(8,128)(2,1)S(1)}, u32[]{:S(2)}, u32[]{:S(2)}) collective-permute-start(bf16[256,256]{1,0:T(8,128)(2,1)S(1)} %constant_dynamic-slice_fusion), channel_id=1, source_target_pairs={{0,1},{1,0},{2,3},{3,2},{4,5},{5,4},{6,7},{7,6},{8,9},{9,8},{10,11... | collective-permute-start | bytes 393224 | tf_op jit(solution)/shard_map/ppermute | solution.py:299
  (20 other events, 108.2 us)
Sparse Core Ops, SparseCore 0:
  68.7 87.4 all-gather.8
  158.1 59.3 all-gather.10
  219.3 53.4 all-gather.12
  274.4 53.4 all-gather.14
